TPU v7x, 128 devices: a whole 4x4x4 slice. The times are simulated.
128 devices in a mesh: rep: 4 (over y_hi, core), grp: 16 (over z, x), tp: 2 (over y_lo).
Axes of the slice: x: 4, y: 4 (y_hi: 2, y_lo: 2; y = y_hi * 2 + y_lo), z: 4, core: 2. Of those that a mesh axis runs over, the one named last changes fastest.
Arguments:
- tokens: bfloat16 [8, 2048, 2048], P('rep', 'grp'), may hold values from -6 to 6
- cotangent: bfloat16 [8, 2048, 2048], P('rep', 'grp'), may hold values from -6 to 6
- offsets: int32 [8, 16], P('rep'), may hold values from 0 to 1920, as said below
- w_query: float32 [2048, 2048], P('grp', 'tp'), may hold values from -0.125 to 0.125
- moment_query: float32 [2048, 2048], P('grp', 'tp'), may hold values from -112 to 112
- square_query: float32 [2048, 2048], P('grp', 'tp'), may hold values from 1310.72 to 9175.04
- w_keyval: float32 [2048, 2, 256], P('grp', None, 'tp'), may hold values from -0.125 to 0.125
- moment_keyval: float32 [2048, 2, 256], P('grp', None, 'tp'), may hold values from -112 to 112
- square_keyval: float32 [2048, 2, 256], P('grp', None, 'tp'), may hold values from 1310.72 to 9175.04
- w_out: float32 [2048, 2048], P('grp', 'tp'), may hold values from -4 to 4
- moment_out: float32 [2048, 2048], P('grp', 'tp'), may hold values from -4 to 4
- square_out: float32 [2048, 2048], P('grp', 'tp'), may hold values from 1.28 to 8.96
- w_gateup: float32 [2048, 2, 5632], P('grp', None, 'tp'), may hold values from -0.125 to 0.125
- moment_gateup: float32 [2048, 2, 5632], P('grp', None, 'tp'), may hold values from -28 to 28
- square_gateup: float32 [2048, 2, 5632], P('grp', None, 'tp'), may hold values from 72.0896 to 507.904
- w_down: float32 [2048, 5632], P('grp', 'tp'), may hold values from -0.078125 to 0.078125
- moment_down: float32 [2048, 5632], P('grp', 'tp'), may hold values from -48 to 48
- square_down: float32 [2048, 5632], P('grp', 'tp'), may hold values from 235.9296 to 1638.4
- norm_gains: float32 [2048, 2], P('grp'), may hold values from 0.5 to 1.5
- moment_gains: float32 [2048, 2], P('grp'), may hold values from -96 to 96
- square_gains: float32 [2048, 2], P('grp'), may hold values from 950.272 to 6553.6
Outputs:
- layer_out: bfloat16 [8, 2048, 2048], P('rep', 'grp')
- input_grad: float32 [8, 2048, 2048], P('rep', 'grp')
- new_query: float32 [2048, 2048], P('grp', 'tp')
- new_moment_query: float32 [2048, 2048], P('grp', 'tp')
- new_square_query: float32 [2048, 2048], P('grp', 'tp')
- new_keyval: float32 [2048, 2, 256], P('grp', None, 'tp')
- new_moment_keyval: float32 [2048, 2, 256], P('grp', None, 'tp')
- new_square_keyval: float32 [2048, 2, 256], P('grp', None, 'tp')
- new_out: float32 [2048, 2048], P('grp', 'tp')
- new_moment_out: float32 [2048, 2048], P('grp', 'tp')
- new_square_out: float32 [2048, 2048], P('grp', 'tp')
- new_gateup: float32 [2048, 2, 5632], P('grp', None, 'tp')
- new_moment_gateup: float32 [2048, 2, 5632], P('grp', None, 'tp')
- new_square_gateup: float32 [2048, 2, 5632], P('grp', None, 'tp')
- new_down: float32 [2048, 5632], P('grp', 'tp')
- new_moment_down: float32 [2048, 5632], P('grp', 'tp')
- new_square_down: float32 [2048, 5632], P('grp', 'tp')
- new_gains: float32 [2048, 2], P('grp')
- new_moment_gains: float32 [2048, 2], P('grp')
- new_square_gains: float32 [2048, 2], P('grp')
Inputs may be any that keep to these rules, and one draw needn't show every extreme that they name: `offsets`: in each row the entries are the multiples 0, 128, ..., 1920, each once, in an order drawn per sequence.
All inputs are finite; a program needn't handle non-finite values.
Results may differ from a plain program's by a relative error of at most 0.024.
Values may be sent and summed in bfloat16 or wider, within the bound.
No kernel may reach another device: no remote copies, remote signals or barrier semaphores. Data moves between devices by JAX's collectives and lax.ppermute only.
A program may use at most 320 MiB of HBM per device.

v0:
```python
import jax
import jax.numpy as jnp
from jax import lax
from jax.sharding import PartitionSpec as P

D = 2048
HEAD_DIM = 64
FF = 5632
LENGTH = 2048
STEP = 10


norm_epsilon = 1e-05
rope_base = 10000.0
neg_large = -1e30
beta_first = 0.9
beta_second = 0.95
adam_epsilon = 1e-08
decay_rate = 0.1


def rope_tables(positions):
    half_dim = HEAD_DIM // 2
    inverse = rope_base ** (-2.0 * jnp.arange(half_dim, dtype=jnp.float32) / HEAD_DIM)
    angles = positions.astype(jnp.float32)[:, None] * inverse[None, :]
    return (jnp.cos(angles)[:, None, :], jnp.sin(angles)[:, None, :])


def rotate(vector, cosine_table, sine_table):
    half_dim = vector.shape[-1] // 2
    first_half = vector[..., :half_dim]
    second_half = vector[..., half_dim:]
    return jnp.concatenate(
        [
            first_half * cosine_table - second_half * sine_table,
            second_half * cosine_table + first_half * sine_table,
        ],
        axis=-1,
    )


def rotate_back(vector, cosine_table, sine_table):
    half_dim = vector.shape[-1] // 2
    first_half = vector[..., :half_dim]
    second_half = vector[..., half_dim:]
    return jnp.concatenate(
        [
            first_half * cosine_table + second_half * sine_table,
            second_half * cosine_table - first_half * sine_table,
        ],
        axis=-1,
    )


def norm_back(upstream, gain, normed, scale):
    weighted = upstream * gain
    return scale * (weighted - normed * jnp.mean(weighted * normed, axis=-1, keepdims=True))


def adamw(weight, moment, square, grad, rate, decay):
    moment = beta_first * moment + (1.0 - beta_first) * grad
    square = beta_second * square + (1.0 - beta_second) * grad * grad
    fix_first = 1.0 - beta_first**STEP
    fix_second = 1.0 - beta_second**STEP
    update = moment / fix_first / (jnp.sqrt(square / fix_second) + adam_epsilon)
    return (weight * (1.0 - rate * decay) - rate * update, moment, square)


def on_device(
    tokens,
    cotangent,
    offsets,
    w_query,
    moment_query,
    square_query,
    w_keyval,
    moment_keyval,
    square_keyval,
    w_out,
    moment_out,
    square_out,
    w_gateup,
    moment_gateup,
    square_gateup,
    w_down,
    moment_down,
    square_down,
    norm_gains,
    moment_gains,
    square_gains,
):
    sequences, own_len, model_width = tokens.shape
    row_count = sequences * own_len
    group_size = lax.axis_size("grp")
    group_place = lax.axis_index("grp")
    seq_len = own_len * group_size
    own_rows = w_query.shape[0]
    local_heads = w_query.shape[1] // HEAD_DIM
    local_kv = w_keyval.shape[2] // HEAD_DIM
    head_ratio = local_heads // local_kv
    local_units = w_down.shape[1]
    steps_in = jnp.arange(own_len, dtype=jnp.int32)
    query_pos = lax.dynamic_slice_in_dim(offsets, group_place, 1, 1) + steps_in[None, :]
    key_pos = (offsets[:, :, None] + steps_in[None, None, :]).reshape(sequences, seq_len)
    cosine_table, sine_table = rope_tables(query_pos.reshape(row_count))
    local_attn = (
        w_query.astype(jnp.bfloat16),
        w_keyval.astype(jnp.bfloat16),
        w_out.astype(jnp.bfloat16),
        norm_gains.astype(jnp.bfloat16),
    )
    local_mlp = (w_gateup.astype(jnp.bfloat16), w_down.astype(jnp.bfloat16))
    full_query, full_keyval, full_out, full_gains = (
        lax.all_gather(local_attn[0], "grp", axis=0, tiled=True),
        lax.all_gather(local_attn[1], "grp", axis=0, tiled=True),
        lax.all_gather(local_attn[2], "grp", axis=0, tiled=True),
        lax.all_gather(local_attn[3], "grp", axis=0, tiled=True),
    )
    full_gateup, full_down = (
        lax.all_gather(local_mlp[0], "grp", axis=0, tiled=True),
        lax.all_gather(local_mlp[1], "grp", axis=0, tiled=True),
    )
    inputs = tokens.reshape(row_count, model_width).astype(jnp.float32)
    gain_one = full_gains[:, 0].astype(jnp.float32)
    gain_two = full_gains[:, 1].astype(jnp.float32)
    scale_one = lax.rsqrt(jnp.mean(inputs * inputs, axis=-1, keepdims=True) + norm_epsilon)
    normed_one = inputs * scale_one
    h_one = (normed_one * gain_one).astype(jnp.bfloat16)
    query_pre = jnp.dot(h_one, full_query, preferred_element_type=jnp.float32)
    keyval_pre = jnp.einsum("td,dcj->tcj", h_one, full_keyval, preferred_element_type=jnp.float32)
    queries = (
        rotate(query_pre.reshape(row_count, local_heads, HEAD_DIM), cosine_table, sine_table)
        * HEAD_DIM ** (-0.5)
    ).astype(jnp.bfloat16)
    keys = rotate(
        keyval_pre[:, 0].reshape(row_count, local_kv, HEAD_DIM), cosine_table, sine_table
    ).astype(jnp.bfloat16)
    values = keyval_pre[:, 1].astype(jnp.bfloat16)
    all_keys, all_values = (
        lax.all_gather(
            keys.reshape(sequences, own_len, local_kv * HEAD_DIM), "grp", axis=1, tiled=True
        ),
        lax.all_gather(
            values.reshape(sequences, own_len, local_kv * HEAD_DIM), "grp", axis=1, tiled=True
        ),
    )
    query_seq = queries.reshape(sequences, own_len, local_kv, head_ratio, HEAD_DIM)
    key_seq = all_keys.reshape(sequences, seq_len, local_kv, HEAD_DIM)
    value_seq = all_values.reshape(sequences, seq_len, local_kv, HEAD_DIM)

    def masked_scores(query_one, key_one, own_pos, other_pos):
        scores = jnp.einsum(
            "qhgd,khd->hgqk", query_one, key_one, preferred_element_type=jnp.float32
        )
        allowed = other_pos[None, :] <= own_pos[:, None]
        return jnp.where(allowed, scores, neg_large)

    def attend(pieces):
        query_one, key_one, value_one, own_pos, other_pos = pieces
        scores = masked_scores(query_one, key_one, own_pos, other_pos)
        row_max = jnp.max(scores, axis=-1, keepdims=True)
        exponent = jnp.exp(scores - row_max)
        row_total = jnp.sum(exponent, axis=-1, keepdims=True)
        attn_probs = (exponent / row_total).astype(jnp.bfloat16)
        mixed_one = jnp.einsum(
            "hgqk,khd->qhgd", attn_probs, value_one, preferred_element_type=jnp.float32
        ).astype(jnp.bfloat16)
        return (mixed_one, (row_max + jnp.log(row_total))[..., 0])

    mixed_heads, log_totals = lax.map(attend, (query_seq, key_seq, value_seq, query_pos, key_pos))
    mixed_flat = mixed_heads.reshape(row_count, local_heads * HEAD_DIM)
    attn_part = lax.dot_general(
        mixed_flat, full_out, (((1,), (1,)), ((), ())), preferred_element_type=jnp.float32
    )
    middle = inputs + lax.psum(attn_part, "tp")
    scale_two = lax.rsqrt(jnp.mean(middle * middle, axis=-1, keepdims=True) + norm_epsilon)
    normed_two = middle * scale_two
    h_two = (normed_two * gain_two).astype(jnp.bfloat16)
    gate_up = jnp.einsum("td,dcf->tcf", h_two, full_gateup, preferred_element_type=jnp.float32)
    gate_pre = gate_up[:, 0]
    up_value = gate_up[:, 1]
    sigmoid_gate = jax.nn.sigmoid(gate_pre)
    activated = gate_pre * sigmoid_gate
    hidden = (activated * up_value).astype(jnp.bfloat16)
    mlp_part = lax.dot_general(
        hidden, full_down, (((1,), (1,)), ((), ())), preferred_element_type=jnp.float32
    )
    result = middle + lax.psum(mlp_part.astype(jnp.bfloat16), "tp").astype(jnp.float32)
    layer_out = result.astype(jnp.bfloat16).reshape(sequences, own_len, model_width)
    back_query, back_keyval, back_out, back_gains = (
        lax.all_gather(local_attn[0], "grp", axis=0, tiled=True),
        lax.all_gather(local_attn[1], "grp", axis=0, tiled=True),
        lax.all_gather(local_attn[2], "grp", axis=0, tiled=True),
        lax.all_gather(local_attn[3], "grp", axis=0, tiled=True),
    )
    back_gateup, back_down = (
        lax.all_gather(local_mlp[0], "grp", axis=0, tiled=True),
        lax.all_gather(local_mlp[1], "grp", axis=0, tiled=True),
    )
    back_one = back_gains[:, 0].astype(jnp.float32)
    back_two = back_gains[:, 1].astype(jnp.float32)
    grad_low = cotangent.reshape(row_count, model_width)
    grad_hidden = jnp.dot(grad_low, back_down, preferred_element_type=jnp.float32)
    grad_gate = grad_hidden * up_value * (sigmoid_gate * (1.0 + gate_pre * (1.0 - sigmoid_gate)))
    grad_up = grad_hidden * activated
    grad_gateup = jnp.stack([grad_gate, grad_up], axis=1).astype(jnp.bfloat16)
    part_two = jnp.einsum(
        "tcf,dcf->td", grad_gateup, back_gateup, preferred_element_type=jnp.float32
    )
    grad_h_two = lax.psum(part_two, "tp")
    grad_gain_two = jnp.sum(grad_h_two * normed_two, axis=0)
    grad_middle = grad_low.astype(jnp.float32) + norm_back(
        grad_h_two, back_two, normed_two, scale_two
    )
    grad_attn = grad_middle.astype(jnp.bfloat16)
    grad_mixed = jnp.dot(grad_attn, back_out, preferred_element_type=jnp.float32).astype(
        jnp.bfloat16
    )
    grad_seq = grad_mixed.reshape(sequences, own_len, local_kv, head_ratio, HEAD_DIM)

    def attend_back(pieces):
        query_one, key_one, value_one, own_pos, other_pos, totals_one, grad_one = pieces
        scores = masked_scores(query_one, key_one, own_pos, other_pos)
        attn_probs = jnp.exp(scores - totals_one[..., None])
        probs_low = attn_probs.astype(jnp.bfloat16)
        grad_probs = jnp.einsum(
            "qhgd,khd->hgqk", grad_one, value_one, preferred_element_type=jnp.float32
        )
        inner_sum = jnp.sum(attn_probs * grad_probs, axis=-1, keepdims=True)
        grad_scores = (attn_probs * (grad_probs - inner_sum)).astype(jnp.bfloat16)
        grad_query = jnp.einsum(
            "hgqk,khd->qhgd", grad_scores, key_one, preferred_element_type=jnp.float32
        )
        grad_key = jnp.einsum(
            "hgqk,qhgd->khd", grad_scores, query_one, preferred_element_type=jnp.float32
        )
        grad_value = jnp.einsum(
            "hgqk,qhgd->khd", probs_low, grad_one, preferred_element_type=jnp.float32
        )
        return (grad_query, grad_key, grad_value)

    grad_query, grad_key, grad_value = lax.map(
        attend_back, (query_seq, key_seq, value_seq, query_pos, key_pos, log_totals, grad_seq)
    )
    own_key, own_value = (
        lax.psum_scatter(
            grad_key.reshape(sequences, seq_len, local_kv * HEAD_DIM).astype(jnp.bfloat16),
            "grp",
            scatter_dimension=1,
            tiled=True,
        ).astype(jnp.float32),
        lax.psum_scatter(
            grad_value.reshape(sequences, seq_len, local_kv * HEAD_DIM).astype(jnp.bfloat16),
            "grp",
            scatter_dimension=1,
            tiled=True,
        ).astype(jnp.float32),
    )
    grad_query_low = (
        (
            rotate_back(
                grad_query.reshape(row_count, local_heads, HEAD_DIM), cosine_table, sine_table
            )
            * HEAD_DIM ** (-0.5)
        )
        .astype(jnp.bfloat16)
        .reshape(row_count, local_heads * HEAD_DIM)
    )
    grad_key_low = (
        rotate_back(own_key.reshape(row_count, local_kv, HEAD_DIM), cosine_table, sine_table)
        .astype(jnp.bfloat16)
        .reshape(row_count, local_kv * HEAD_DIM)
    )
    grad_value_low = own_value.reshape(row_count, local_kv * HEAD_DIM).astype(jnp.bfloat16)
    grad_keyval = jnp.stack([grad_key_low, grad_value_low], axis=1)
    part_one = lax.dot_general(
        grad_query_low, back_query, (((1,), (1,)), ((), ())), preferred_element_type=jnp.float32
    )
    part_one = part_one + jnp.einsum(
        "tcj,dcj->td", grad_keyval, back_keyval, preferred_element_type=jnp.float32
    )
    grad_h_one = lax.psum(part_one.astype(jnp.bfloat16), "tp").astype(jnp.float32)
    grad_gain_one = jnp.sum(grad_h_one * normed_one, axis=0)
    input_grad = (grad_middle + norm_back(grad_h_one, back_one, normed_one, scale_one)).reshape(
        sequences, own_len, model_width
    )
    right_one = jnp.concatenate(
        [grad_query_low, grad_keyval.reshape(row_count, 2 * local_kv * HEAD_DIM)], axis=1
    )
    right_two = grad_gateup.reshape(row_count, 2 * local_units)

    def product(left, right):
        return lax.dot_general(
            left, right, (((0,), (0,)), ((), ())), preferred_element_type=jnp.float32
        )

    owner_sums = lax.psum_scatter(
        jnp.concatenate(
            [
                product(h_one, right_one),
                product(grad_attn, mixed_flat),
                product(h_two, right_two),
                product(grad_low, hidden),
            ],
            axis=1,
        ).astype(jnp.bfloat16),
        "grp",
        scatter_dimension=0,
        tiled=True,
    ).astype(jnp.float32)
    gain_terms = jnp.stack([grad_gain_one, grad_gain_two], axis=1)
    gain_total = lax.psum(gain_terms, ("rep", "grp"))
    grad_gains = lax.dynamic_slice_in_dim(gain_total, group_place * own_rows, own_rows, 0)
    reduced = lax.psum(owner_sums, "rep")
    query_cols = local_heads * HEAD_DIM
    keyval_cols = 2 * local_kv * HEAD_DIM
    edge_two = query_cols + keyval_cols
    edge_three = edge_two + query_cols
    edge_four = edge_three + 2 * local_units
    grad_wq = reduced[:, :query_cols]
    grad_wkv = reduced[:, query_cols:edge_two].reshape(own_rows, 2, local_kv * HEAD_DIM)
    grad_wo = reduced[:, edge_two:edge_three]
    grad_wgu = reduced[:, edge_three:edge_four].reshape(own_rows, 2, local_units)
    grad_wd = reduced[:, edge_four:]
    rate_wide = 2.0 * D ** (-0.5)
    rate_out = 2.0 * max(1, 2 * D // LENGTH) ** (-0.5)
    rate_down = 2.0 * FF ** (-0.5)
    new_query, new_moment_query, new_square_query = adamw(
        w_query, moment_query, square_query, grad_wq, rate_wide, decay_rate
    )
    new_keyval, new_moment_keyval, new_square_keyval = adamw(
        w_keyval, moment_keyval, square_keyval, grad_wkv, rate_wide, decay_rate
    )
    new_out, new_moment_out, new_square_out = adamw(
        w_out, moment_out, square_out, grad_wo, rate_out, decay_rate
    )
    new_gateup, new_moment_gateup, new_square_gateup = adamw(
        w_gateup, moment_gateup, square_gateup, grad_wgu, rate_wide, decay_rate
    )
    new_down, new_moment_down, new_square_down = adamw(
        w_down, moment_down, square_down, grad_wd, rate_down, decay_rate
    )
    new_gains, new_moment_gains, new_square_gains = adamw(
        norm_gains, moment_gains, square_gains, grad_gains, 1.0, 0.0
    )
    return (
        layer_out,
        input_grad,
        new_query,
        new_moment_query,
        new_square_query,
        new_keyval,
        new_moment_keyval,
        new_square_keyval,
        new_out,
        new_moment_out,
        new_square_out,
        new_gateup,
        new_moment_gateup,
        new_square_gateup,
        new_down,
        new_moment_down,
        new_square_down,
        new_gains,
        new_moment_gains,
        new_square_gains,
    )


def solution(mesh):
    in_specs = (
        P("rep", "grp", None),
        P("rep", "grp", None),
        P("rep", None),
        P("grp", "tp"),
        P("grp", "tp"),
        P("grp", "tp"),
        P("grp", None, "tp"),
        P("grp", None, "tp"),
        P("grp", None, "tp"),
        P("grp", "tp"),
        P("grp", "tp"),
        P("grp", "tp"),
        P("grp", None, "tp"),
        P("grp", None, "tp"),
        P("grp", None, "tp"),
        P("grp", "tp"),
        P("grp", "tp"),
        P("grp", "tp"),
        P("grp", None),
        P("grp", None),
        P("grp", None),
    )
    out_specs = (
        P("rep", "grp", None),
        P("rep", "grp", None),
        P("grp", "tp"),
        P("grp", "tp"),
        P("grp", "tp"),
        P("grp", None, "tp"),
        P("grp", None, "tp"),
        P("grp", None, "tp"),
        P("grp", "tp"),
        P("grp", "tp"),
        P("grp", "tp"),
        P("grp", None, "tp"),
        P("grp", None, "tp"),
        P("grp", None, "tp"),
        P("grp", "tp"),
        P("grp", "tp"),
        P("grp", "tp"),
        P("grp", None),
        P("grp", None),
        P("grp", None),
    )
    return jax.shard_map(
        on_device, mesh=mesh, in_specs=in_specs, out_specs=out_specs, check_vma=False
    )
```

profile of v0, /device:TPU:1, one launch (start us, length us, event | category | flops | bytes accessed | tf_op | source)
XLA Modules:
  0.0 1725.7 jit_solution(3627071977385353599)
XLA Ops:
  9.8 18.2 %all_gather.30 = bf16[2048,2]{0,1:T(2,128)(2,1)S(1)} all-gather(bf16[128,2]{0,1:T(2,128)(2,1)S(1)} %convert_element_type.189), channel_id=1, replica_groups=mesh['rep'=4,'grp'=16,'tp'=2] {'grp'}, dimensions={0}, use_global_device_ids=true | all-gather | bytes 8704 | tf_op jit(solution)/shard_map/all_gather | solution.py:117
  32.6 22.8 %all-gather.8.cloned.1.call-done = bf16[2048,2,128]{2,0,1:T(8,128)(2,1)} async-done(((bf16[128,2,128]{2,0,1:T(8,128)(2,1)}), bf16[2048,2,128]{2,0,1:T(8,128)(2,1)}) %all-gather.8.cloned.1.call-update) | async-done | bytes 1048592 | tf_op jit(solution)/shard_map/all_gather | solution.py:115
  64.8 50.6 %all-gather.12.cloned.1.call-done = bf16[2,2048,128]{1,0,2:T(2,128)(2,1)} async-done(((bf16[2,128,128]{1,0,2:T(2,128)(2,1)}), bf16[2,2048,128]{1,0,2:T(2,128)(2,1)}) %all-gather.12.cloned.1.call-update) | async-done | bytes 1048592 | tf_op jit(solution)/shard_map/all_gather | solution.py:140
  116.9 44.4 %all-gather.10.cloned.1.call-done = bf16[2,2048,128]{2,1,0:T(8,128)(2,1)} async-done(((bf16[2,128,128]{2,1,0:T(8,128)(2,1)}), bf16[2,2048,128]{2,1,0:T(8,128)(2,1)}) %all-gather.10.cloned.1.call-update) | async-done | bytes 1048592 | tf_op jit(solution)/shard_map/all_gather | solution.py:143
  162.8 53.5 %all-gather.14.cloned.1.call-done = bf16[2048,1024]{1,0:T(8,128)(2,1)} async-done(((bf16[128,1024]{1,0:T(8,128)(2,1)}), bf16[2048,1024]{1,0:T(8,128)(2,1)}) %all-gather.14.cloned.1.call-update) | async-done | bytes 4194320 | tf_op jit(solution)/shard_map/all_gather | solution.py:114
  216.3 6.5 copy.93
  222.8 3.8 fusion.112
  229.4 52.4 %while.26 = (s32[]{:T(128)}, bf16[2,128,2,8,64]{1,4,3,2,0:T(8,128)(2,1)}, f32[2,2,8,128]{3,2,1,0:T(8,128)S(1)}, bf16[2,2048,2,64]{1,3,2,0:T(8,128)(2,1)S(1)}, s3...) while((s32[]{:T(128)}, ...), condition=%wide.region_4.5_spmd, body=%wide.region_1.4_spmd.sunk | while | flops 1111881728 | bytes 57241256 | solution.py:170
  229.8 8.2 fusion.153
  238.0 8.7 fusion.154
  246.7 8.1 fusion.155
  256.0 8.3 fusion.153
  264.3 8.8 fusion.154
  273.1 7.8 fusion.155
  283.9 5.0 fusion.94
  289.0 3.2 copy.147
  293.2 64.9 %all-reduce.6.cloned.1.call-done = f32[256,2048]{1,0:T(8,128)} async-done(((f32[256,2048]{1,0:T(8,128)}), f32[256,2048]{1,0:T(8,128)}) %all-reduce.6.cloned.1.call-update) | async-done | bytes 2097168 | tf_op jit(solution)/shard_map/psum | solution.py:175
  358.1 2.2 multiply_reduce_fusion.2
  360.3 145.3 %all-gather.18.cloned.1.call-done = bf16[2048,2,2816]{2,0,1:T(8,128)(2,1)} async-done(((bf16[128,2,2816]{2,0,1:T(8,128)(2,1)}), bf16[2048,2,2816]{2,0,1:T(8,128)(2,1)}) %all-gather.18.cloned.1.call-update) | async-done | bytes 23068688 | tf_op jit(solution)/shard_map/all_gather | solution.py:120
  505.6 13.3 fusion.84
  518.9 74.7 %all-gather.20.cloned.1.call-done = bf16[2048,2816]{1,0:T(8,128)(2,1)} async-done(((bf16[128,2816]{1,0:T(8,128)(2,1)}), bf16[2048,2816]{1,0:T(8,128)(2,1)}) %all-gather.20.cloned.1.call-update) | async-done | bytes 11534352 | tf_op jit(solution)/shard_map/all_gather | solution.py:121
  593.6 11.4 fusion.60
  604.9 12.5 convolution_bitcast_fusion.2
  617.6 3.6 maximum_convert_fusion
  621.2 4.5 copy.107
  625.7 61.0 %all-reduce.8.cloned.1.call-done = f32[256,2048]{1,0:T(8,128)} async-done(((f32[256,2048]{1,0:T(8,128)}), f32[256,2048]{1,0:T(8,128)}) %all-reduce.8.cloned.1.call-update) | async-done | bytes 2097168 | tf_op jit(solution)/shard_map/psum | solution.py:210
  686.7 3.0 multiply_reduce_fusion
  697.6 106.7 %while.27 = (s32[]{:T(128)}, f32[2,128,2,8,64]{1,0,4,3,2:T(2,128)}, bf16[2,2048,2,64]{1,3,2,0:T(8,128)(2,1)}, bf16[2,2048,2,64]{1,3,2,0:T(8,128)(2,1)}, bf16[2,2...) while((s32[]{:T(128)}, f32[2,128,2,8,64]{1,0,4,3,2:T(2,128)}, ...), condition=%wide.region_12.13_spmd, body=%wide.region_10.12_spmd.sunk | while | flops 2734946304 | bytes 242308880 | solution.py:242
  697.8 2.4 fusion.164
  700.6 10.4 fusion.166
  711.0 8.1 fusion.167
  722.4 13.1 dynamic_update_slice.32
  735.5 6.9 fusion.169
  742.4 7.7 fusion.170
  751.1 2.4 fusion.164
  753.9 10.4 fusion.166
  764.2 8.1 fusion.167
  775.6 13.1 dynamic_update_slice.32
  788.7 6.9 fusion.169
  795.6 7.7 fusion.170
  804.3 2.3 copy.103
  806.6 103.0 %copy.124 = bf16[2,2048,128]{0,2,1:T(8,128)(2,1)} copy(bf16[2,2048,128]{1,0,2:T(2,128)(2,1)S(1)} %bitcast.339) | data formatting | bytes 2097152
  909.6 97.1 %reshape.318 = bf16[2048,256]{1,0:T(8,128)(2,1)} reshape(bf16[2048,128,2]{2,1,0:T(8,128)(2,1)} %bitcast.74) | data formatting | bytes 2097152
  1006.9 10.3 convolution_convert_fusion.3
  1017.2 12.9 convolution_convert_fusion
  1030.1 2.3 copy.104
  1032.5 9.0 convert_bitcast_fusion
  1043.6 5.1 convolution_convert_fusion.2
  1048.7 6.4 copy.110
  1056.2 23.2 %reduce-scatter.10.cloned.1.call-done = bf16[128,256]{1,0:T(8,128)(2,1)} async-done(((bf16[2048,256]{1,0:T(8,128)(2,1)}), bf16[128,256]{1,0:T(8,128)(2,1)}) %reduce-scatter.10.cloned.1.call-update) | async-done | bytes 65552
  1079.4 10.8 reshape.319
  1090.1 6.2 copy.125
  1096.6 59.2 %reduce-scatter.6.cloned.1.call-done = bf16[2,128,128]{2,1,0:T(8,128)(2,1)} async-done(((bf16[2,2048,128]{2,1,0:T(8,128)(2,1)}), bf16[2,128,128]{2,1,0:T(8,128)(2,1)}) %reduce-scatter.6.cloned.1.call-update) | async-done | bytes 65552 | tf_op jit(solution)/shard_map/reduce_scatter | solution.py:252
  1156.8 4.9 convolution_convert_fusion.1
  1161.7 7.9 copy.109
  1170.7 4.5 fusion.66
  1175.3 29.9 %pad_maximum_fusion = bf16[2048,10752]{1,0:T(8,128)(2,1)} fusion(bf16[2048,2816]{1,0:T(8,128)(2,1)} %convert_bitcast_fusion, bf16[2048,5632]{1,0:T(8,128)(2,1)} %convolution_convert_fusion, bf16[2048,1024]{1,0:T(8,128)(2,1)} %copy.110, bf16[2048,1280]{1,0:T(8,128)(2,1)} %copy.109), kind=kLoop, calls=%fused_computation.67 | loop fusion | flops 176160768 | bytes 88080384 | tf_op jit(solution)/shard_map/concatenate | solution.py:298
  1205.3 40.6 %all-reduce.10.cloned.1.call-done = (bf16[256,2048]{1,0:T(8,128)(2,1)}, bf16[256,2048]{1,0:T(8,128)(2,1)}) async-done(((bf16[256,2048]{1,0:T(8,128)(2,1)}, bf16[256,2048]{1,0:T(8,128)(2,1)}), (bf16[256,2048]{1,0:T(8,128)(2,1)}, bf16[256,2048]{1,0:T(8,128)(2,1)})) %all-reduce.10.cloned.1.call-update) | async-done | bytes 2097168 | tf_op jit(solution)/shard_map/psum | solution.py:188
  1248.0 304.2 %psum.47 = f32[2048,2]{0,1:T(2,128)S(1)} all-reduce(f32[2048,2]{0,1:T(2,128)S(1)} %pad_maximum_fusion.4), channel_id=1, replica_groups=mesh['rep'=4,'grp'=16,'tp'=2] {'rep','grp'}, use_global_device_ids=true, to_apply=%region_21.22 | all-reduce | flops 4096 | bytes 32768 | tf_op jit(solution)/shard_map/psum | solution.py:312
  1552.9 5.0 fusion.71
  1557.8 134.4 %all-reduce.11 = f32[128,10752]{1,0:T(8,128)} all-reduce(bf16[128,10752]{1,0:T(8,128)(2,1)} %reduce-scatter.8.cloned.1.call-done), channel_id=1, replica_groups=mesh['rep'=4,'grp'=16,'tp'=2] {'rep'}, use_global_device_ids=true, to_apply=%region_18.19 | all-reduce | flops 1376256 | bytes 8257536 | tf_op jit(solution)/shard_map/psum | solution.py:314
  1694.2 3.0 reshape.300
  1697.2 5.5 multiply_subtract_fusion.1
  1704.4 12.3 multiply_subtract_fusion
  (244 shorter events, 58.9 us)
Async XLA Ops:
  7.2 48.2 %all-gather.8.cloned.1.call-start = ((), (), s32[]{:S(2)}) async-start(), calls=%async_computation.3 | async-start | bytes 1114112 | tf_op jit(solution)/shard_map/all_gather | solution.py:115
  8.8 106.5 %all-gather.12.cloned.1.call-start = ((), (), s32[]{:S(2)}) async-start(), calls=%async_computation.5 | async-start | bytes 1114112 | tf_op jit(solution)/shard_map/all_gather | solution.py:140
  30.3 196.3 %copy-start.30 = (f32[256,32]{0,1:T(8,128)}, f32[256,32]{0,1:T(8,128)S(1)}, u32[]{:S(2)}) copy-start(f32[256,32]{0,1:T(8,128)S(1)} %get-tuple-element.259) | copy-start | bytes 98308
  30.3 196.3 %copy-start.32 = (f32[256,32]{0,1:T(8,128)}, f32[256,32]{0,1:T(8,128)S(1)}, u32[]{:S(2)}) copy-start(f32[256,32]{0,1:T(8,128)S(1)} %get-tuple-element.260) | copy-start | bytes 98308
  30.9 32.6 %copy-start.44 = (f32[2048,1]{0,1:T(1,128)}, f32[2048,1]{0,1:T(1,128)S(1)}, u32[]{:S(2)}) copy-start(f32[2048,1]{0,1:T(1,128)S(1)} %get-tuple-element.258) | copy-start | bytes 24580
  30.9 30.8 %copy-start.21 = (f32[128,1024]{1,0:T(8,128)S(1)}, f32[128,1024]{1,0:T(8,128)}, u32[]{:S(2)}) copy-start(f32[128,1024]{1,0:T(8,128)} %param.28) | copy-start | bytes 1572868
  32.5 30.8 %copy-start.14 = (bf16[256,2048]{1,0:T(8,128)(2,1)}, bf16[256,2048]{1,0:T(8,128)(2,1)S(1)}, u32[]{:S(2)}) copy-start(bf16[256,2048]{1,0:T(8,128)(2,1)S(1)} %fusion.75) | copy-start | bytes 3145732
  32.5 30.1 %copy-start.23 = (f32[128,1024]{1,0:T(8,128)S(1)}, f32[128,1024]{1,0:T(8,128)}, u32[]{:S(2)}) copy-start(f32[128,1024]{1,0:T(8,128)} %param.34) | copy-start | bytes 1572868
  32.5 31.0 %copy-start.8 = (bf16[2,128,2048]{2,1,0:T(8,128)(2,1)S(1)}, bf16[2,128,2048]{2,1,0:T(8,128)(2,1)}, u32[]{:S(2)}) copy-start(bf16[2,128,2048]{2,1,0:T(8,128)(2,1)} %param.25) | copy-start | bytes 3145732
  61.0 100.4 %all-gather.10.cloned.1.call-start = ((), (), s32[]{:S(2)}) async-start(), calls=%async_computation.4 | async-start | bytes 1114112 | tf_op jit(solution)/shard_map/all_gather | solution.py:143
  61.7 154.6 %all-gather.14.cloned.1.call-start = ((), (), s32[]{:S(2)}) async-start(), calls=%async_computation.6 | async-start | bytes 4456448 | tf_op jit(solution)/shard_map/all_gather | solution.py:114
  62.5 221.3 %all-gather.16.cloned.1.call-start = ((), (), s32[]{:S(2)}) async-start(), calls=%async_computation.7 | async-start | bytes 4456448 | tf_op jit(solution)/shard_map/all_gather | solution.py:116
  63.4 294.7 %all-reduce.6.cloned.1.call-start = ((), (), s32[]{:S(2)}) async-start(), calls=%async_computation.8 | async-start | bytes 4194304 | tf_op jit(solution)/shard_map/psum | solution.py:175
  238.0 8.7 copy-start.41
  264.3 8.8 copy-start.41
  281.8 7.1 copy-start.6
  281.8 7.0 copy-start.11
  283.8 5.0 copy-start.19
  288.9 216.7 %all-gather.18.cloned.1.call-start = ((), (), s32[]{:S(2)}) async-start(), calls=%async_computation.9 | async-start | bytes 24510464 | tf_op jit(solution)/shard_map/all_gather | solution.py:120
  292.2 301.4 %all-gather.20.cloned.1.call-start = ((), (), s32[]{:S(2)}) async-start(), calls=%async_computation.10 | async-start | bytes 12255232 | tf_op jit(solution)/shard_map/all_gather | solution.py:121
  293.2 212.5 %copy-start.34 = (f32[2048,1]{0,1:T(1,128)S(1)}, f32[2048,1]{0,1:T(1,128)}, u32[]{:S(2)}) copy-start(f32[2048,1]{0,1:T(1,128)} %get-tuple-element.257) | copy-start | bytes 24580
  293.2 393.5 %all-reduce.8.cloned.1.call-start = ((), (), s32[]{:S(2)}) async-start(), calls=%async_computation.11 | async-start | bytes 4194304 | tf_op jit(solution)/shard_map/psum | solution.py:210
  360.3 329.4 %copy-start.4 = (f32[256,2048]{1,0:T(8,128)}, f32[256,2048]{1,0:T(8,128)S(1)}, u32[]{:S(2)}) copy-start(f32[256,2048]{1,0:T(8,128)S(1)} %get-tuple-element.239) | copy-start | bytes 6291460
  360.3 329.4 %copy-start.48 = (f32[256]{0:T(256)}, f32[256]{0:T(256)S(1)}, u32[]{:S(2)}) copy-start(f32[256]{0:T(256)S(1)} %add_rsqrt_fusion) | copy-start | bytes 3076
  617.5 461.9 %reduce-scatter.10.cloned.1.call-start = ((), (), s32[]{:S(2)}) async-start(), calls=%async_computation.14 | async-start | bytes 1114112
  693.9 3.7 copy-start.7
  700.2 10.8 copy-start.2
  719.1 3.3 copy-start.3
  735.5 6.9 copy-start.28
  753.4 10.8 copy-start.2
  788.7 6.9 copy-start.28
  1006.8 10.4 copy-start.5
  1006.8 10.3 copy-start.35
  1006.8 10.3 copy-start.49
  1006.8 149.0 %reduce-scatter.6.cloned.1.call-start = ((), (), s32[]{:S(2)}) async-start(), calls=%async_computation.12 | async-start | bytes 1114112 | tf_op jit(solution)/shard_map/reduce_scatter | solution.py:252
  1032.4 213.5 %all-reduce.10.cloned.1.call-start = ((), (), s32[]{:S(2)}) async-start(), calls=%async_computation.15 | async-start | bytes 4194304 | tf_op jit(solution)/shard_map/psum | solution.py:188
  1048.7 6.4 copy-start.31
  1048.7 6.4 copy-start.33
  1090.1 66.7 %copy-start.15 = (bf16[256,2048]{1,0:T(8,128)(2,1)S(1)}, bf16[256,2048]{1,0:T(8,128)(2,1)}, u32[]{:S(2)}) copy-start(bf16[256,2048]{1,0:T(8,128)(2,1)} %copy-done.14) | copy-start | bytes 3145732
  1161.7 7.9 copy-start.18
  1161.7 7.9 copy-start.43
  1175.2 382.6 %reduce-scatter.8.cloned.1.call-start = ((), (), s32[]{:S(2)}) async-start(), calls=%async_computation.13 | async-start | bytes 46792704 | tf_op jit(solution)/shard_map/reduce_scatter | solution.py:297
  1205.2 40.7 %copy-start.9 = (bf16[2,128,2048]{2,1,0:T(8,128)(2,1)S(1)}, bf16[2,128,2048]{2,1,0:T(8,128)(2,1)}, u32[]{:S(2)}) copy-start(bf16[2,128,2048]{2,1,0:T(8,128)(2,1)} %param.25) | copy-start | bytes 3145732
  1205.2 40.7 %copy-start.45 = (f32[2048,1]{0,1:T(1,128)S(1)}, f32[2048,1]{0,1:T(1,128)}, u32[]{:S(2)}) copy-start(f32[2048,1]{0,1:T(1,128)} %copy-done.44) | copy-start | bytes 24580
  1205.2 40.7 %copy-start.52 = (f32[256]{0:T(256)S(1)}, f32[256]{0:T(256)}, u32[]{:S(2)}) copy-start(f32[256]{0:T(256)} %copy-done.51) | copy-start | bytes 3076
  1205.2 42.8 %copy-start.50 = (f32[2048]{0:T(1024)S(1)}, f32[2048]{0:T(1024)}, u32[]{:S(2)}) copy-start(f32[2048]{0:T(1024)} %get-tuple-element.176) | copy-start | bytes 24580
  1205.2 347.0 %copy-start.53 = (f32[128,2]{0,1:T(2,128)S(1)}, f32[128,2]{0,1:T(2,128)}, u32[]{:S(2)}) copy-start(f32[128,2]{0,1:T(2,128)} %param.43) | copy-start | bytes 3076
  1205.3 347.0 %copy-start.54 = (f32[128,2]{0,1:T(2,128)S(1)}, f32[128,2]{0,1:T(2,128)}, u32[]{:S(2)}) copy-start(f32[128,2]{0,1:T(2,128)} %param.44) | copy-start | bytes 3076
  1205.3 347.0 %copy-start.55 = (f32[128,2]{0,1:T(2,128)S(1)}, f32[128,2]{0,1:T(2,128)}, u32[]{:S(2)}) copy-start(f32[128,2]{0,1:T(2,128)} %param.45) | copy-start | bytes 3076
  1697.2 5.5 copy-start.40
  1697.2 5.5 copy-start.46
  1697.2 5.5 copy-start.47
  1697.2 6.7 copy-start.12
  1697.2 6.7 copy-start.13
  1697.2 7.1 copy-start.20
  1702.7 14.0 slice-start
  1704.3 12.4 slice-start.1
  1704.3 12.4 copy-start.22
  1704.3 12.4 copy-start.24
  1704.3 12.4 copy-start.36
  1704.3 12.4 copy-start.37
  1704.3 12.4 copy-start.38
  1704.3 12.4 copy-start.39
  1704.4 14.6 copy-start.1
  (17 other events, 33.4 us)
Sparse Core Ops, SparseCore 0:
  10.8 44.5 all-gather.7
  61.1 54.2 all-gather.11
  118.1 43.2 all-gather.9
  163.9 52.3 all-gather.13
  218.9 51.2 all-gather.15
  289.0 69.0 all-reduce.5
  361.0 144.5 all-gather.17
  508.6 84.9 all-gather.19
  617.6 69.0 all-reduce.7
  1006.9 72.4 reduce-scatter.9
  1083.5 72.2 reduce-scatter.5
  1175.3 70.5 all-reduce.9
  1249.9 252.5 reduce-scatter.7
where the time goes:
time: 1740 us; the launch traced here: 1730 us
  waiting for transfers between devices  640 us (37%)
  blocking collectives  457 us (26%)
  local copies, waits for them, and re-layouts  310 us (18%)
  matrix products  186 us (11%)
  other arithmetic  116 us (7%)
    psum x1, blocking collectives, on_device(): gain_total = lax.psum(gain_terms, ('rep', 'grp'))  304 us
    unnamed x115, local copies, waits for them, and re-layouts  225 us
    all_gather x1, waiting for transfers between devices, on_device(): lax.all_gather(local_mlp[0], 'grp', axis=0, tiled=True)  145 us
    psum x1, blocking collectives, on_device(): reduced = lax.psum(owner_sums, 'rep')  134 us
    all_gather x1, waiting for transfers between devices, on_device(): lax.all_gather(local_mlp[1], 'grp', axis=0, tiled=True)  74.7 us
    psum x1, waiting for transfers between devices, on_device(): middle = inputs + lax.psum(attn_part, 'tp')  64.9 us
    psum x1, waiting for transfers between devices, on_device(): grad_h_two = lax.psum(part_two, 'tp')  61 us
    reduce_scatter x1, waiting for transfers between devices, on_device(): lax.psum_scatter(grad_value.reshape(sequences, seq_len, local_kv * HEAD_D...  59.2 us
  transfers between devices with their start and end apart: 13, of which 11 were waited for; matrix products, arithmetic and copies ran while one was open for 12% of the time, Pallas kernels for 0%

commit v1 on v0

v1 whole, which is shorter than its diff:
```python
import functools

import jax
import jax.numpy as jnp
from jax import lax
from jax.experimental import pallas as pl
from jax.experimental.pallas import tpu as pltpu
from jax.sharding import PartitionSpec as P

D = 2048
HEAD_DIM = 64
FF = 5632
LENGTH = 2048
STEP = 10
GROUP = 16
SPAN = 128
TILE = 128

norm_epsilon = 1e-05
rope_base = 10000.0
neg_large = -1e30
beta_first = 0.9
beta_second = 0.95
adam_epsilon = 1e-08
decay_rate = 0.1

bf16 = jnp.bfloat16
f32 = jnp.float32

VMEM_LIMIT = 56 * 1024 * 1024

CORE_SWAP = [(0, 1), (1, 0), (2, 3), (3, 2)]
REPLICA_SWAP = [(0, 2), (1, 3), (2, 0), (3, 1)]
TP_SWAP = [(0, 1), (1, 0)]


def params():
    return pltpu.CompilerParams(vmem_limit_bytes=VMEM_LIMIT)


def dot_nn(left, right):
    return lax.dot_general(left, right, (((1,), (0,)), ((), ())), preferred_element_type=f32)


def dot_nt(left, right):
    return lax.dot_general(left, right, (((1,), (1,)), ((), ())), preferred_element_type=f32)


def dot_tn(left, right):
    return lax.dot_general(left, right, (((0,), (0,)), ((), ())), preferred_element_type=f32)


def adamw(weight, moment, square, grad, rate, decay):
    moment = beta_first * moment + (1.0 - beta_first) * grad
    square = beta_second * square + (1.0 - beta_second) * grad * grad
    fix_first = 1.0 - beta_first**STEP
    fix_second = 1.0 - beta_second**STEP
    update = moment / fix_first / (jnp.sqrt(square / fix_second) + adam_epsilon)
    return (weight * (1.0 - rate * decay) - rate * update, moment, square)


def norm_back(upstream, gain, normed, scale):
    weighted = upstream * gain
    return scale * (weighted - normed * jnp.mean(weighted * normed, axis=-1, keepdims=True))


def partner(values):
    lane = lax.broadcasted_iota(jnp.int32, values.shape, 1)
    up = pltpu.roll(values, 96, 1)
    down = pltpu.roll(values, 32, 1)
    return jnp.where(lane % HEAD_DIM < HEAD_DIM // 2, up, down)


def row_of(block):
    return jnp.concatenate([block[i : i + 1, :] for i in range(GROUP)], axis=1)


def project_kernel(x_ref, wq_ref, wkv_ref, gain_ref, cos_ref, sin_ref, h_ref, q_ref, kv_ref):
    x = x_ref[...].astype(f32)
    scale = lax.rsqrt(jnp.mean(x * x, axis=-1, keepdims=True) + norm_epsilon)
    gain = row_of(gain_ref[:, 0, :].astype(f32))
    h = (x * scale * gain).astype(bf16)
    h_ref[...] = h
    cos = cos_ref[...]
    sin = sin_ref[...]
    lane = lax.broadcasted_iota(jnp.int32, (SPAN, 128), 1)
    low_half = lane < HEAD_DIM
    query = dot_nn(h, wq_ref[...].reshape(D, 512))
    for pair in range(4):
        block = query[:, pair * 128 : (pair + 1) * 128]
        turned = (block * cos + partner(block) * sin) * (HEAD_DIM**-0.5)
        q_ref[2 * pair] = jnp.where(low_half, turned, 0.0).astype(bf16)
        q_ref[2 * pair + 1] = jnp.where(
            low_half, pltpu.roll(turned, HEAD_DIM, 1), 0.0
        ).astype(bf16)
    keyval = dot_nn(h, wkv_ref[...].reshape(D, 128))
    turned = keyval * cos + partner(keyval) * sin
    kv_ref[...] = jnp.where(low_half, turned, keyval).astype(bf16)


def project(x, attn_full, cos, sin):
    rows = x.shape[0]
    row = lambda i: (i, 0)
    return pl.pallas_call(
        project_kernel,
        grid=(rows // SPAN,),
        in_specs=[
            pl.BlockSpec((SPAN, D), row),
            pl.BlockSpec((GROUP, 128, 512), lambda i: (0, 0, 0)),
            pl.BlockSpec((GROUP, 128, 128), lambda i: (0, 0, 8)),
            pl.BlockSpec((GROUP, 16, 128), lambda i: (0, 8, 0)),
            pl.BlockSpec((SPAN, 128), row),
            pl.BlockSpec((SPAN, 128), row),
        ],
        out_specs=[
            pl.BlockSpec((SPAN, D), row),
            pl.BlockSpec((8, SPAN, 128), lambda i: (0, i, 0)),
            pl.BlockSpec((SPAN, 128), row),
        ],
        out_shape=[
            jax.ShapeDtypeStruct((rows, D), bf16),
            jax.ShapeDtypeStruct((8, rows, 128), bf16),
            jax.ShapeDtypeStruct((rows, 128), bf16),
        ],
        compiler_params=params(),
        name="project",
    )(x, attn_full, attn_full, attn_full, cos, sin)


CHUNK = 512


def causal_offsets():
    key = lax.broadcasted_iota(jnp.int32, (128, 256), 0)
    query = lax.broadcasted_iota(jnp.int32, (128, 256), 1) % SPAN
    return key - query


def attend_kernel(off_ref, place_ref, q_ref, kv_ref, wo_ref, o_ref, lse_ref, part_ref, kvt, score):
    seq = pl.program_id(0)
    kv = kv_ref[...].reshape(LENGTH, 128)
    kvt[...] = kv.T
    own = off_ref[seq, place_ref[0]]
    differ = causal_offsets()

    def pair_step(pair, carry):
        q = q_ref[pl.ds(2 * pair, 2)].reshape(256, 128)
        top = jnp.full((1, 256), neg_large, f32)
        for c in range(LENGTH // CHUNK):
            raw = dot_nt(kv_ref[4 * c : 4 * c + 4].reshape(CHUNK, 128), q)
            for j in range(CHUNK // 128):
                block = raw[j * 128 : (j + 1) * 128]
                block = jnp.where(differ <= own - off_ref[seq, 4 * c + j], block, neg_large)
                score[c * CHUNK + j * 128 : c * CHUNK + (j + 1) * 128, :] = block
                top = jnp.maximum(top, jnp.max(block, axis=0, keepdims=True))
        total = jnp.zeros((1, 256), f32)
        mixed = jnp.zeros((128, 256), f32)
        for c in range(LENGTH // CHUNK):
            weight = jnp.exp(score[c * CHUNK : (c + 1) * CHUNK, :] - top)
            total = total + jnp.sum(weight, axis=0, keepdims=True)
            mixed = mixed + dot_nn(kvt[:, c * CHUNK : (c + 1) * CHUNK], weight.astype(bf16))
        out = (mixed[HEAD_DIM:, :] / total).T
        o_ref[pair] = jnp.concatenate([out[:SPAN], out[SPAN:]], axis=1).astype(bf16)
        lse = top + jnp.log(total)
        lse_ref[0, pl.ds(pair, 1), :] = lse
        return carry

    lax.fori_loop(0, 4, pair_step, 0)
    heads = jnp.concatenate([o_ref[i] for i in range(4)], axis=1)
    part_ref[...] = dot_nt(heads, wo_ref[...].reshape(D, 512)).astype(bf16)


def attend(offsets, place, q, kv_all, attn_full):
    rows = q.shape[1]
    seqs = rows // SPAN
    grid_spec = pltpu.PrefetchScalarGridSpec(
        num_scalar_prefetch=2,
        grid=(seqs,),
        in_specs=[
            pl.BlockSpec((8, SPAN, 128), lambda i, *_: (0, i, 0)),
            pl.BlockSpec((GROUP, SPAN, 128), lambda i, *_: (0, i, 0)),
            pl.BlockSpec((GROUP, 128, 512), lambda i, *_: (0, 0, 1)),
        ],
        out_specs=[
            pl.BlockSpec((4, SPAN, 128), lambda i, *_: (0, i, 0)),
            pl.BlockSpec((1, 4, 256), lambda i, *_: (i, 0, 0)),
            pl.BlockSpec((SPAN, D), lambda i, *_: (i, 0)),
        ],
        scratch_shapes=[pltpu.VMEM((128, LENGTH), bf16), pltpu.VMEM((LENGTH, 256), f32)],
    )
    return pl.pallas_call(
        attend_kernel,
        grid_spec=grid_spec,
        out_shape=[
            jax.ShapeDtypeStruct((4, rows, 128), bf16),
            jax.ShapeDtypeStruct((seqs, 4, 256), f32),
            jax.ShapeDtypeStruct((rows, D), bf16),
        ],
        compiler_params=params(),
        name="attend",
    )(offsets, place, q, kv_all, attn_full)


def mlp_kernel(h_ref, dy_ref, w_ref, side_ref, out_ref, back_ref, out_sum, back_sum):
    step = pl.program_id(0)

    @pl.when(step == 0)
    def _():
        out_sum[...] = jnp.zeros_like(out_sum)
        back_sum[...] = jnp.zeros_like(back_sum)

    w_gu = w_ref[:, : 2 * TILE]
    w_d = w_ref[:, 2 * TILE :]
    both = dot_nn(h_ref[...], w_gu)
    upstream = dot_nn(dy_ref[...], w_d)
    gate = both[:, :TILE]
    up = both[:, TILE:]
    sigmoid = jax.nn.sigmoid(gate)
    active = gate * sigmoid
    hidden = (active * up).astype(bf16)
    d_gate = (upstream * up * (sigmoid * (1.0 + gate * (1.0 - sigmoid)))).astype(bf16)
    d_up = (upstream * active).astype(bf16)
    d_both = jnp.concatenate([d_gate, d_up], axis=1)
    side_ref[:, : 2 * TILE] = d_both
    side_ref[:, 2 * TILE :] = hidden
    out_sum[...] += dot_nt(hidden, w_d)
    back_sum[...] += dot_nt(d_both, w_gu)

    @pl.when(step == pl.num_programs(0) - 1)
    def _():
        out_ref[...] = out_sum[...].astype(bf16)
        back_ref[...] = back_sum[...].astype(bf16)


def mlp(h, dy, w_full):
    rows = h.shape[0]
    width = 3 * TILE
    steps = w_full.shape[1] // width
    whole = pl.BlockSpec((rows, D), lambda i: (0, 0))
    return pl.pallas_call(
        mlp_kernel,
        grid=(steps,),
        in_specs=[whole, whole, pl.BlockSpec((D, width), lambda i: (0, i))],
        out_specs=[pl.BlockSpec((rows, width), lambda i: (0, i)), whole, whole],
        out_shape=[
            jax.ShapeDtypeStruct((rows, steps * width), bf16),
            jax.ShapeDtypeStruct((rows, D), bf16),
            jax.ShapeDtypeStruct((rows, D), bf16),
        ],
        scratch_shapes=[pltpu.VMEM((rows, D), f32), pltpu.VMEM((rows, D), f32)],
        compiler_params=params(),
        name="mlp",
    )(h, dy, w_full)


def mlp_grads_kernel(h_ref, dy_ref, side_ref, out_ref):
    out_ref[:, : 2 * TILE] = dot_nn(h_ref[...], side_ref[:, : 2 * TILE]).astype(bf16)
    out_ref[:, 2 * TILE :] = dot_nn(dy_ref[...], side_ref[:, 2 * TILE :]).astype(bf16)


def mlp_grads(h_t, dy_t, side):
    rows = side.shape[0]
    width = 3 * TILE
    steps = side.shape[1] // width
    whole = pl.BlockSpec((D, rows), lambda i: (0, 0))
    return pl.pallas_call(
        mlp_grads_kernel,
        grid=(steps,),
        in_specs=[whole, whole, pl.BlockSpec((rows, width), lambda i: (0, i))],
        out_specs=pl.BlockSpec((D, width), lambda i: (0, i)),
        out_shape=jax.ShapeDtypeStruct((D, steps * width), bf16),
        compiler_params=params(),
        name="mlp_grads",
    )(h_t, dy_t, side)


def attend_back_kernel(
    off_ref, place_ref, da_ref, wo_ref, q_ref, kv_ref, o_ref, lse_ref, cos_ref, sin_ref,
    dq_ref, dkv_ref, kvt, d_heads, dkv,
):
    seq = pl.program_id(0)
    kvt[...] = kv_ref[...].reshape(LENGTH, 128).T
    dkv[...] = jnp.zeros_like(dkv)
    d_all = dot_nn(da_ref[...], wo_ref[...].reshape(D, 512))
    for pair in range(4):
        d_heads[pair] = d_all[:, pair * 128 : (pair + 1) * 128].astype(bf16).astype(f32)
    own = off_ref[seq, place_ref[0]]
    differ = causal_offsets()
    lane = lax.broadcasted_iota(jnp.int32, (SPAN, 128), 1)
    high_half = lane >= HEAD_DIM
    cos = cos_ref[...]
    sin = sin_ref[...]

    def pair_step(pair, carry):
        q = q_ref[pl.ds(2 * pair, 2)].reshape(256, 128)
        d_out = d_heads[pair]
        first = jnp.where(high_half, pltpu.roll(d_out, HEAD_DIM, 1), 0.0).astype(bf16)
        second = jnp.where(high_half, d_out, 0.0).astype(bf16)
        d_o = jnp.concatenate([first, second], axis=0)
        dots = (d_out * o_ref[pair].astype(f32)).T
        inner = jnp.concatenate(
            [
                jnp.sum(dots[:HEAD_DIM], axis=0, keepdims=True),
                jnp.sum(dots[HEAD_DIM:], axis=0, keepdims=True),
            ],
            axis=1,
        )
        lse = lse_ref[0, pl.ds(pair, 1), :]
        d_query = jnp.zeros((128, 256), f32)
        for c in range(LENGTH // CHUNK):
            kv = kv_ref[4 * c : 4 * c + 4].reshape(CHUNK, 128)
            raw = dot_nt(kv, q)
            parts = []
            for j in range(CHUNK // 128):
                block = raw[j * 128 : (j + 1) * 128]
                parts.append(
                    jnp.where(differ <= own - off_ref[seq, 4 * c + j], block, neg_large)
                )
            prob = jnp.exp(jnp.concatenate(parts, axis=0) - lse)
            d_prob = dot_nt(kv, d_o)
            d_score = (prob * (d_prob - inner)).astype(bf16)
            span = slice(c * CHUNK, (c + 1) * CHUNK)
            dkv[span, :] += dot_nn(d_score, q) + dot_nn(prob.astype(bf16), d_o)
            d_query = d_query + dot_nn(kvt[:, span], d_score)
        turned = d_query[:HEAD_DIM, :].T
        block = jnp.concatenate([turned[:SPAN], turned[SPAN:]], axis=1)
        block = (block * cos - partner(block) * sin) * (HEAD_DIM**-0.5)
        dq_ref[pair] = block.astype(bf16)
        return carry

    lax.fori_loop(0, 4, pair_step, 0)
    dkv_ref[...] = dkv[...].astype(bf16).reshape(GROUP, SPAN, 128)


def attend_back(offsets, place, da, attn_full, q, kv_all, o, lse, cos, sin):
    rows = da.shape[0]
    seqs = rows // SPAN
    grid_spec = pltpu.PrefetchScalarGridSpec(
        num_scalar_prefetch=2,
        grid=(seqs,),
        in_specs=[
            pl.BlockSpec((SPAN, D), lambda i, *_: (i, 0)),
            pl.BlockSpec((GROUP, 128, 512), lambda i, *_: (0, 0, 1)),
            pl.BlockSpec((8, SPAN, 128), lambda i, *_: (0, i, 0)),
            pl.BlockSpec((GROUP, SPAN, 128), lambda i, *_: (0, i, 0)),
            pl.BlockSpec((4, SPAN, 128), lambda i, *_: (0, i, 0)),
            pl.BlockSpec((1, 4, 256), lambda i, *_: (i, 0, 0)),
            pl.BlockSpec((SPAN, 128), lambda i, *_: (i, 0)),
            pl.BlockSpec((SPAN, 128), lambda i, *_: (i, 0)),
        ],
        out_specs=[
            pl.BlockSpec((4, SPAN, 128), lambda i, *_: (0, i, 0)),
            pl.BlockSpec((GROUP, SPAN, 128), lambda i, *_: (0, i, 0)),
        ],
        scratch_shapes=[
            pltpu.VMEM((128, LENGTH), bf16),
            pltpu.VMEM((4, SPAN, 128), f32),
            pltpu.VMEM((LENGTH, 128), f32),
        ],
    )
    return pl.pallas_call(
        attend_back_kernel,
        grid_spec=grid_spec,
        out_shape=[
            jax.ShapeDtypeStruct((4, rows, 128), bf16),
            jax.ShapeDtypeStruct((GROUP, rows, 128), bf16),
        ],
        compiler_params=params(),
        name="attend_back",
    )(offsets, place, da, attn_full, q, kv_all, o, lse, cos, sin)


def project_back_kernel(
    dq_ref, dkv_ref, wq_ref, wkv_ref, x_ref, cos_ref, sin_ref, dh_ref, right_ref, gain_ref
):
    lane = lax.broadcasted_iota(jnp.int32, (SPAN, 128), 1)
    total = jnp.sum(dkv_ref[...].astype(f32), axis=0)
    turned = total * cos_ref[...] - partner(total) * sin_ref[...]
    d_kv = jnp.where(lane < HEAD_DIM, turned, total).astype(bf16)
    d_q = jnp.concatenate([dq_ref[i] for i in range(4)], axis=1)
    right_ref[:, :512] = d_q
    right_ref[:, 512:] = d_kv
    d_h = dot_nt(d_q, wq_ref[...].reshape(D, 512)) + dot_nt(d_kv, wkv_ref[...].reshape(D, 128))
    dh_ref[...] = d_h.astype(bf16)
    x = x_ref[...].astype(f32)
    scale = lax.rsqrt(jnp.mean(x * x, axis=-1, keepdims=True) + norm_epsilon)
    terms = (d_h * (x * scale)).reshape(SPAN // 8, 8, D).sum(axis=0)

    @pl.when(pl.program_id(0) == 0)
    def _():
        gain_ref[...] = jnp.zeros_like(gain_ref)

    gain_ref[...] += terms


def project_back(dq, dkv, attn_full, x, cos, sin):
    rows = x.shape[0]
    row = lambda i: (i, 0)
    return pl.pallas_call(
        project_back_kernel,
        grid=(rows // SPAN,),
        in_specs=[
            pl.BlockSpec((4, SPAN, 128), lambda i: (0, i, 0)),
            pl.BlockSpec((GROUP, SPAN, 128), lambda i: (0, i, 0)),
            pl.BlockSpec((GROUP, 128, 512), lambda i: (0, 0, 0)),
            pl.BlockSpec((GROUP, 128, 128), lambda i: (0, 0, 8)),
            pl.BlockSpec((SPAN, D), row),
            pl.BlockSpec((SPAN, 128), row),
            pl.BlockSpec((SPAN, 128), row),
        ],
        out_specs=[
            pl.BlockSpec((SPAN, D), row),
            pl.BlockSpec((SPAN, 640), row),
            pl.BlockSpec((8, D), lambda i: (0, 0)),
        ],
        out_shape=[
            jax.ShapeDtypeStruct((rows, D), bf16),
            jax.ShapeDtypeStruct((rows, 640), bf16),
            jax.ShapeDtypeStruct((8, D), f32),
        ],
        compiler_params=params(),
        name="project_back",
    )(dq, dkv, attn_full, attn_full, x, cos, sin)


def attn_grads_kernel(h_ref, right_ref, da_ref, o_ref, gain_ref, out_ref):
    first = dot_tn(h_ref[...], right_ref[...]).astype(bf16)
    heads = jnp.concatenate([o_ref[i] for i in range(4)], axis=1)
    out_ref[0, :128, :512] = first[:, :512]
    out_ref[0, :128, 512:1024] = dot_tn(da_ref[...], heads).astype(bf16)
    out_ref[0, :128, 1024:] = first[:, 512:]
    out_ref[0, 128:, :] = jnp.zeros((16, 1152), bf16)
    out_ref[0, 128:, :128] = gain_ref[...].astype(bf16)


def attn_grads(h, right, da, o, gains):
    rows = h.shape[0]
    column = lambda g: (0, g)
    return pl.pallas_call(
        attn_grads_kernel,
        grid=(GROUP,),
        in_specs=[
            pl.BlockSpec((rows, 128), column),
            pl.BlockSpec((rows, 640), lambda g: (0, 0)),
            pl.BlockSpec((rows, 128), column),
            pl.BlockSpec((4, rows, 128), lambda g: (0, 0, 0)),
            pl.BlockSpec((16, 128), column),
        ],
        out_specs=pl.BlockSpec((1, 144, 1152), lambda g: (g, 0, 0)),
        out_shape=jax.ShapeDtypeStruct((GROUP, 144, 1152), bf16),
        compiler_params=params(),
        name="attn_grads",
    )(h, right, da, o, gains)


def pack_kernel(core_ref, gu_ref, d_ref, out_ref):
    out_ref[:, :TILE] = gu_ref[:, 0, :].astype(bf16)
    out_ref[:, TILE : 2 * TILE] = gu_ref[:, 1, :].astype(bf16)
    out_ref[:, 2 * TILE :] = d_ref[...].astype(bf16)


def pack_mlp(core, w_gateup, w_down):
    rows, units = w_down.shape
    tiles = units // 2 // TILE
    grid_spec = pltpu.PrefetchScalarGridSpec(
        num_scalar_prefetch=1,
        grid=(tiles,),
        in_specs=[
            pl.BlockSpec((rows, 2, TILE), lambda i, core: (0, 0, core[0] * tiles + i)),
            pl.BlockSpec((rows, TILE), lambda i, core: (0, core[0] * tiles + i)),
        ],
        out_specs=pl.BlockSpec((rows, 3 * TILE), lambda i, core: (0, i)),
    )
    return pl.pallas_call(
        pack_kernel,
        grid_spec=grid_spec,
        out_shape=jax.ShapeDtypeStruct((rows, tiles * 3 * TILE), bf16),
        compiler_params=params(),
        name="pack_mlp",
    )(core, w_gateup, w_down)


def mlp_adam_kernel(
    core_ref, own_ref, other_ref, wg, mg, sg, wd, md, sd, wg_o, mg_o, sg_o, wd_o, md_o, sd_o,
    *, tiles, rate_wide, rate_down,
):
    mine = pl.program_id(0) // tiles == core_ref[0]
    grad = jnp.where(mine, own_ref[...].astype(f32), other_ref[...].astype(f32))
    for i in range(2):
        new = adamw(
            wg[:, i, :], mg[:, i, :], sg[:, i, :], grad[:, i * TILE : (i + 1) * TILE],
            rate_wide, decay_rate,
        )
        wg_o[:, i, :], mg_o[:, i, :], sg_o[:, i, :] = new
    new = adamw(wd[...], md[...], sd[...], grad[:, 2 * TILE :], rate_down, decay_rate)
    wd_o[...], md_o[...], sd_o[...] = new


def mlp_adam(core, own, other, gateup, down, rate_wide, rate_down):
    rows, units = down[0].shape
    tiles = units // 2 // TILE
    wide = pl.BlockSpec((rows, 2, TILE), lambda i, core: (0, 0, i))
    flat = pl.BlockSpec((rows, TILE), lambda i, core: (0, i))
    grad = pl.BlockSpec((rows, 3 * TILE), lambda i, core: (0, i % tiles))
    grid_spec = pltpu.PrefetchScalarGridSpec(
        num_scalar_prefetch=1,
        grid=(2 * tiles,),
        in_specs=[grad, grad] + [wide] * 3 + [flat] * 3,
        out_specs=[wide] * 3 + [flat] * 3,
    )
    shapes = [jax.ShapeDtypeStruct(gateup[0].shape, f32)] * 3
    shapes += [jax.ShapeDtypeStruct(down[0].shape, f32)] * 3
    return pl.pallas_call(
        functools.partial(
            mlp_adam_kernel, tiles=tiles, rate_wide=rate_wide, rate_down=rate_down
        ),
        grid_spec=grid_spec,
        out_shape=shapes,
        compiler_params=params(),
        name="mlp_adam",
    )(core, own, other, *gateup, *down)


def swap_core(values):
    return lax.ppermute(values, "rep", CORE_SWAP)


def swap_replica(values):
    return lax.ppermute(values, "rep", REPLICA_SWAP)


def swap_tp(values):
    return lax.ppermute(values, "tp", TP_SWAP)


def sum_shares(part, own_rows):
    from_core = swap_core(part[own_rows:])
    share = (part[:own_rows].astype(f32) + from_core.astype(f32)).astype(bf16)
    return share.astype(f32) + swap_tp(share).astype(f32)


def on_device(
    tokens,
    cotangent,
    offsets,
    w_query,
    moment_query,
    square_query,
    w_keyval,
    moment_keyval,
    square_keyval,
    w_out,
    moment_out,
    square_out,
    w_gateup,
    moment_gateup,
    square_gateup,
    w_down,
    moment_down,
    square_down,
    norm_gains,
    moment_gains,
    square_gains,
):
    sequences, own_len, width = tokens.shape
    own_rows = sequences * own_len
    core = lax.axis_index("rep") % 2
    core_list = core.reshape(1).astype(jnp.int32)
    place = lax.axis_index("grp").reshape(1).astype(jnp.int32)
    first_core = core == 0

    def half(values):
        size = values.shape[-1] // 2
        return jnp.where(first_core, values[..., :size], values[..., size:])

    def whole(own, other):
        return jnp.concatenate(
            [jnp.where(first_core, own, other), jnp.where(first_core, other, own)], axis=-1
        )

    keyval_half = half(w_keyval)
    attn_pack = jnp.concatenate(
        [half(w_query), half(w_out), keyval_half[:, 0], keyval_half[:, 1]], axis=1
    ).astype(bf16)
    gain_rows = jnp.pad(norm_gains.astype(bf16).T, ((0, 14), (0, 1024)))
    attn_pack = jnp.concatenate([attn_pack, gain_rows], axis=0)
    attn_full = lax.all_gather(attn_pack, "grp", axis=0, tiled=False)
    mlp_full = lax.all_gather(pack_mlp(core_list, w_gateup, w_down), "grp", axis=0, tiled=True)

    x_own = tokens.reshape(own_rows, width)
    dy_own = cotangent.reshape(own_rows, width)
    x_all = jnp.concatenate([x_own, swap_core(x_own)], axis=0)
    dy_all = jnp.concatenate([dy_own, swap_core(dy_own)], axis=0)
    offsets_all = jnp.concatenate([offsets, swap_core(offsets)], axis=0)
    steps_in = jnp.arange(own_len, dtype=jnp.int32)
    starts = lax.dynamic_slice_in_dim(offsets_all, place[0], 1, 1)
    positions = (starts + steps_in[None, :]).reshape(2 * own_rows)
    half_dim = HEAD_DIM // 2
    inverse = rope_base ** (-2.0 * jnp.arange(half_dim, dtype=f32) / HEAD_DIM)
    angles = positions.astype(f32)[:, None] * inverse[None, :]
    cos_part = jnp.cos(angles)
    sin_part = jnp.sin(angles)
    cos = jnp.concatenate([cos_part] * 4, axis=1)
    sin = jnp.concatenate([-sin_part, sin_part] * 2, axis=1)

    h_one, q, kv = project(x_all, attn_full, cos, sin)
    kv_all = lax.all_to_all(
        jnp.broadcast_to(kv[None], (GROUP,) + kv.shape), "grp", 0, 0, tiled=False
    )
    o, lse, attn_part = attend(offsets_all, place, q, kv_all, attn_full)
    gains = attn_full[:, 128:130, :128].astype(f32)
    gain_one = gains[:, 0].reshape(1, width)
    gain_two = gains[:, 1].reshape(1, width)

    x_low = x_own.astype(f32)
    middle = x_low + sum_shares(attn_part, own_rows)
    scale_two = lax.rsqrt(jnp.mean(middle * middle, axis=-1, keepdims=True) + norm_epsilon)
    normed_two = middle * scale_two
    h_two_own = (normed_two * gain_two).astype(bf16)
    h_two = jnp.concatenate([h_two_own, swap_core(h_two_own)], axis=0)
    side, out_part, back_part = mlp(h_two, dy_all, mlp_full)
    mlp_sums = mlp_grads(h_two.T, dy_all.T, side)
    mlp_own = lax.psum_scatter(mlp_sums, "grp", scatter_dimension=0, tiled=True)

    grad_h_two = sum_shares(back_part, own_rows)
    grad_gain_two = jnp.sum(grad_h_two * normed_two, axis=0)
    grad_middle = dy_own.astype(f32) + norm_back(grad_h_two, gain_two, normed_two, scale_two)
    da_own = grad_middle.astype(bf16)
    da = jnp.concatenate([da_own, swap_core(da_own)], axis=0)
    layer_out = (middle + sum_shares(out_part, own_rows)).astype(bf16)

    dq, dkv_part = attend_back(offsets_all, place, da, attn_full, q, kv_all, o, lse, cos, sin)
    dkv = lax.all_to_all(dkv_part, "grp", 0, 0, tiled=False)
    dh_part, right, gain_terms = project_back(dq, dkv, attn_full, x_all, cos, sin)
    grad_gain_one = jnp.sum(gain_terms, axis=0)
    gain_grads = jnp.stack([grad_gain_one, 0.5 * grad_gain_two], axis=0)
    gain_grads = jnp.pad(gain_grads, ((0, 14), (0, 0)))
    attn_sums = lax.all_to_all(attn_grads(h_one, right, da, o, gain_grads), "grp", 0, 0)
    attn_own = jnp.sum(attn_sums.astype(f32), axis=0).astype(bf16)

    grad_h_one = sum_shares(dh_part, own_rows)
    scale_one = lax.rsqrt(jnp.mean(x_low * x_low, axis=-1, keepdims=True) + norm_epsilon)
    input_grad = grad_middle + norm_back(grad_h_one, gain_one, x_low * scale_one, scale_one)

    def over_replicas(values):
        return (values.astype(f32) + swap_replica(values).astype(f32)).astype(bf16)

    mlp_total = over_replicas(mlp_own)
    mlp_other = swap_core(mlp_total)
    attn_total = over_replicas(attn_own)
    attn_other = swap_core(attn_total)
    own = attn_total[:128].astype(f32)
    other = attn_other[:128].astype(f32)
    grad_wq = whole(own[:, :512], other[:, :512])
    grad_wo = whole(own[:, 512:1024], other[:, 512:1024])
    grad_wkv = jnp.stack(
        [
            whole(own[:, 1024:1088], other[:, 1024:1088]),
            whole(own[:, 1088:], other[:, 1088:]),
        ],
        axis=1,
    )
    gain_share = attn_total[128:130, :128].astype(f32) + attn_other[128:130, :128].astype(f32)
    grad_gains = (gain_share + swap_tp(gain_share)).T

    rate_wide = 2.0 * D ** (-0.5)
    rate_out = 2.0 * max(1, 2 * D // LENGTH) ** (-0.5)
    rate_down = 2.0 * FF ** (-0.5)
    new_query = adamw(w_query, moment_query, square_query, grad_wq, rate_wide, decay_rate)
    new_keyval = adamw(w_keyval, moment_keyval, square_keyval, grad_wkv, rate_wide, decay_rate)
    new_out = adamw(w_out, moment_out, square_out, grad_wo, rate_out, decay_rate)
    new_mlp = mlp_adam(
        core_list,
        mlp_total,
        mlp_other,
        (w_gateup, moment_gateup, square_gateup),
        (w_down, moment_down, square_down),
        rate_wide,
        rate_down,
    )
    new_gains = adamw(norm_gains, moment_gains, square_gains, grad_gains, 1.0, 0.0)
    return (
        layer_out.reshape(tokens.shape),
        input_grad.reshape(tokens.shape),
        *new_query,
        *new_keyval,
        *new_out,
        *new_mlp,
        *new_gains,
    )


def solution(mesh):
    rows = P("rep", "grp", None)
    flat = P("grp", "tp")
    deep = P("grp", None, "tp")
    states = (flat,) * 3 + (deep,) * 3 + (flat,) * 3 + (deep,) * 3 + (flat,) * 3
    states += (P("grp", None),) * 3
    return jax.shard_map(
        on_device,
        mesh=mesh,
        in_specs=(rows, rows, P("rep", None)) + states,
        out_specs=(rows, rows) + states,
        check_vma=False,
    )
```

time: 1740 us -> 577 us (0.33)
  waiting for transfers between devices: 640 us -> 212 us
  blocking collectives: 457 us -> 50.3 us
  local copies, waits for them, and re-layouts: 310 us -> 48.1 us
  matrix products: 186 us -> 0 us
  Pallas kernels: 0 us -> 172 us
  other arithmetic: 116 us -> 43.2 us
  starting transfers between devices: 0.54 us -> 34.1 us
    psum x2 -> x0, blocking collectives: 439 us -> none  [the longest x1 304 us: on_device(): gain_total = lax.psum(gain_terms, ('rep', 'grp'))]
    all_gather x7 -> x2, waiting for transfers between devices: 391 us -> 42 us  [the longest x1 42 us: on_device(): attn_full = lax.all_gather(attn_pack, 'grp', axis=0, tiled=False)]
    unnamed x115 -> x60, local copies, waits for them, and re-layouts: 225 us -> 9.43 us
    dot_general x28 -> x0, matrix products: 186 us -> none  [the longest x4 31.9 us: product(): lax.dot_general(left, right, (((0,), (0,)), ((), ())), preferred_element_...]
    pallas_call x0 -> x9, Pallas kernels: none -> 172 us  [the longest x1 33.3 us: attend_back(): pl.pallas_call(attend_back_kernel, grid_spec=grid_spec, out_shape=[jax.Sh...]
    psum x3 -> x0, waiting for transfers between devices: 166 us -> none  [the longest x1 64.9 us: on_device(): middle = inputs + lax.psum(attn_part, 'tp')]
    ppermute x0 -> x18, waiting for transfers between devices: none -> 99.3 us  [the longest x5 64.9 us: swap_tp(): return lax.ppermute(values, 'tp', TP_SWAP)]
    all_to_all x0 -> x2, waiting for transfers between devices: none -> 70.4 us  [the longest x1 41.3 us: on_device(): dkv = lax.all_to_all(dkv_part, 'grp', 0, 0, tiled=False)]
  transfers between devices with their start and end apart: 13 -> 23, of which waited for: 11 -> 12; matrix products, arithmetic and copies ran while one was open for 12% -> 15% of each run, Pallas kernels for 0% -> 17%
where the time goes in v1:
time: 577 us; the launch traced here: 574 us
  waiting for transfers between devices  212 us (37%)
  Pallas kernels  172 us (30%)
  blocking collectives  50.3 us (9%)
  local copies, waits for them, and re-layouts  48.1 us (8%)
  other arithmetic  43.2 us (7%)
  starting transfers between devices  34.1 us (6%)
  between operations  14.3 us (2%)
    ppermute x5, waiting for transfers between devices, swap_tp(): return lax.ppermute(values, 'tp', TP_SWAP)  64.9 us
    all_to_all x1, blocking collectives, on_device(): lax.all_to_all(jnp.broadcast_to(kv[None], (GROUP,) + kv.shape), 'grp', 0,...  50.3 us
    all_gather x1, waiting for transfers between devices, on_device(): attn_full = lax.all_gather(attn_pack, 'grp', axis=0, tiled=False)  42 us
    all_to_all x1, waiting for transfers between devices, on_device(): dkv = lax.all_to_all(dkv_part, 'grp', 0, 0, tiled=False)  41.3 us
    pallas_call x1, Pallas kernels, attend_back(): pl.pallas_call(attend_back_kernel, grid_spec=grid_spec, out_shape=[jax.Sh...  33.3 us
    pallas_call x1, Pallas kernels, mlp(): pl.pallas_call(mlp_kernel, grid=(steps,), in_specs=[whole, whole, pl.Bloc...  32 us
    pallas_call x1, Pallas kernels, attend(): pl.pallas_call(attend_kernel, grid_spec=grid_spec, out_shape=[jax.ShapeDt...  30.7 us
    all_to_all x1, waiting for transfers between devices, on_device(): lax.all_to_all(attn_grads(h_one, right, da, o, gain_grads), 'grp', 0, 0)  29.1 us
  transfers between devices with their start and end apart: 23, of which 12 were waited for; matrix products, arithmetic and copies ran while one was open for 15% of the time, Pallas kernels for 17%

profile of v1, /device:TPU:1, one launch (start us, length us, event | category | flops | bytes accessed | tf_op | source)
XLA Modules:
  0.0 573.8 jit_solution(15103598500043486571)
XLA Ops:
  9.0 1.2 select_convert_fusion
  11.2 7.5 %pack_mlp.1 = bf16[128,4224]{1,0:T(8,128)(2,1)} custom-call(s32[1]{0:T(128)} %bitcast.9.core_ref, f32[128,2,2816]{2,1,0:T(2,128)} %wg.1, f32[128,2816]{1,0:T(8,128)} %wd.1), custom_call_target="tpu_custom_call" | custom-call | tf_op jit(solution)/shard_map/pack_mlp/pallas_call | solution.py:474
  19.2 1.5 collective-permute-start.1
  20.8 2.0 collective-permute-done
  24.1 1.3 pad_maximum_fusion.6
  25.4 1.4 pad_maximum_fusion
  26.8 2.4 copy.97.x_ref
  29.2 42.0 %all-gather.6.cloned.1.call-done = bf16[2304,1152]{1,0:T(8,128)(2,1)} async-done(((bf16[144,1152]{1,0:T(8,128)(2,1)}), bf16[2304,1152]{1,0:T(8,128)(2,1)}) %all-gather.6.cloned.1.call-update) | async-done | bytes 5308432 | tf_op jit(solution)/shard_map/all_gather | solution.py:587
  71.2 6.5 %project.1 = (bf16[512,2048]{1,0:T(8,128)(2,1)}, bf16[8,512,128]{2,1,0:T(8,128)(2,1)}, bf16[512,128]{1,0:T(8,128)(2,1)}) custom-call(bf16[512,2048]{1,0:T(8,128)(2,1)} %copy.97.x_ref, bf16[16,144,1152]{2,1,0:T(8,128)(2,1)} %bitcast.36, bf16[16,144,1152]{2,1,0:T(8,128)(2,1)} %bitcast.37, bf16[16,144,1152]{2,1,0:T(8,128)(2,1)} %bitcast.38, ...), custom_call_target="tpu_custom_call" | custom-call | tf_op jit(solution)/shard_map/project/pallas_call | solution.py:104
  77.8 1.3 broadcast_in_dim.2
  79.1 50.3 %all_to_all.15.kv_ref = bf16[16,512,128]{2,1,0:T(8,128)(2,1)} all-to-all(bf16[16,512,128]{2,1,0:T(8,128)(2,1)S(1)} %broadcast_in_dim.2), channel_id=1, replica_groups=mesh['rep'=4,'grp'=16,'tp'=2] {'grp'}, dimensions={0} | all-to-all | bytes 4194304 | tf_op jit(solution)/shard_map/all_to_all | solution.py:607
  129.4 30.7 %attend.1 = (bf16[4,512,128]{2,1,0:T(8,128)(2,1)}, f32[4,4,256]{2,1,0:T(4,128)}, bf16[512,2048]{1,0:T(8,128)(2,1)}) custom-call(s32[4,16]{1,0:T(4,128)} %copy-done.22, s32[1]{0:T(128)} %bitcast.1.place_ref, bf16[8,512,128]{2,1,0:T(8,128)(2,1)} %get-tuple-element.40.q_ref, bf16[16,512,128]{2,1,0:T(8,128)(2,1)} %all_to_all.15.kv_ref, ...), custom_call_target="tpu_custom_call" | custom-call | tf_op jit(solution)/shard_map/attend/pallas_call | solution.py:191
  160.1 2.9 copy.98
  163.1 1.4 collective-permute-start.2
  164.4 2.3 collective-permute-done.2
  166.7 1.2 add_convert_fusion.5
  169.1 2.3 copy.121
  172.9 19.8 %collective-permute-done.3 = bf16[256,2048]{0,1:T(8,128)(2,1)} collective-permute-done((bf16[256,2048]{0,1:T(8,128)(2,1)}, bf16[256,2048]{0,1:T(8,128)(2,1)}, u32[]{:S(2)}, u32[]{:S(2)}) %collective-permute-start.3) | collective-permute-done | bytes 1048608 | tf_op jit(solution)/shard_map/ppermute | solution.py:533
  192.6 2.1 multiply_reduce_fusion.3
  194.7 1.3 multiply_convert_fusion
  197.2 3.5 fusion.18
  200.7 4.0 copy.102.dy_ref
  204.7 3.8 fusion.19
  208.5 3.9 copy.101.h_ref
  212.5 32.0 %mlp.1 = (bf16[512,4224]{1,0:T(8,128)(2,1)}, bf16[512,2048]{1,0:T(8,128)(2,1)}, bf16[512,2048]{1,0:T(8,128)(2,1)}) custom-call(bf16[512,2048]{1,0:T(8,128)(2,1)} %copy.101.h_ref, bf16[512,2048]{1,0:T(8,128)(2,1)} %copy.102.dy_ref, bf16[2048,4224]{1,0:T(8,128)(2,1)} %all-gather.4.cloned.1.call-done.w_ref), custom_call_target="tpu_custom_call" | custom-call | tf_op jit(solution)/shard_map/mlp/pallas_call | solution.py:240
  244.5 17.7 %mlp_grads.1 = bf16[2048,4224]{1,0:T(8,128)(2,1)} custom-call(bf16[2048,512]{1,0:T(8,128)(2,1)} %get-tuple-element.138.h_ref, bf16[2048,512]{1,0:T(8,128)(2,1)} %get-tuple-element.136.dy_ref, bf16[512,4224]{1,0:T(8,128)(2,1)} %get-tuple-element.53.side_ref), custom_call_target="tpu_custom_call" | custom-call | tf_op jit(solution)/shard_map/mlp_grads/pallas_call | solution.py:266
  262.2 3.9 copy.105
  266.2 1.4 slice.137
  267.7 2.6 collective-permute-done.8
  270.7 1.3 collective-permute-start.9
  272.0 23.5 %collective-permute-done.9 = bf16[256,2048]{0,1:T(8,128)(2,1)S(1)} collective-permute-done((bf16[256,2048]{0,1:T(8,128)(2,1)S(1)}, bf16[256,2048]{0,1:T(8,128)(2,1)S(1)}, u32[]{:S(2)}, u32[]{:S(2)}) %collective-permute-start.9) | collective-permute-done | bytes 1048608 | tf_op jit(solution)/shard_map/ppermute | solution.py:533
  296.5 2.1 fusion.17
  299.5 2.3 collective-permute-done.10
  301.8 1.5 pad_maximum_fusion.3
  303.2 4.1 copy.107.da_ref
  307.3 33.3 %attend_back.1 = (bf16[4,512,128]{2,1,0:T(8,128)(2,1)}, bf16[16,512,128]{2,1,0:T(8,128)(2,1)}) custom-call(s32[4,16]{1,0:T(4,128)} %copy-done.22, s32[1]{0:T(128)} %bitcast.1.place_ref, bf16[512,2048]{1,0:T(8,128)(2,1)} %copy.107.da_ref, bf16[16,144,1152]{2,1,0:T(8,128)(2,1)} %bitcast.41, bf16[8,512,128]{2,1,0:T(8,128)(2,1)} %get-tuple-element.40.q_ref, ...), custom_call_target="tpu_custom_call" | custom-call | tf_op jit(solution)/shard_map/attend_back/pallas_call | solution.py:361
  340.6 4.7 all-to-all-start.1
  345.3 41.3 %all-to-all-done.1.dkv_ref = bf16[16,512,128]{2,1,0:T(8,128)(2,1)} async-done(((bf16[16,512,128]{2,1,0:T(8,128)(2,1)}), bf16[16,512,128]{2,1,0:T(8,128)(2,1)}, u32[]{:S(2)}, u32[]{:S(2)}) %all-to-all-start.1) | async-done | bytes 2097184 | tf_op jit(solution)/shard_map/all_to_all | solution.py:633
  386.6 7.9 %project_back.1 = (bf16[512,2048]{1,0:T(8,128)(2,1)}, bf16[512,640]{1,0:T(8,128)(2,1)}, f32[8,2048]{1,0:T(8,128)}) custom-call(bf16[4,512,128]{2,1,0:T(8,128)(2,1)} %get-tuple-element.47.dq_ref, bf16[16,512,128]{2,1,0:T(8,128)(2,1)} %all-to-all-done.1.dkv_ref, bf16[16,144,1152]{2,1,0:T(8,128)(2,1)} %bitcast.42, bf16[16,144,1152]{2,1,0:T(8,128)(2,1)} %bitcast.43, ...), custom_call_target="tpu_custom_call" | custom-call | tf_op jit(solution)/shard_map/project_back/pallas_call | solution.py:399
  396.1 13.7 %attn_grads.1 = bf16[16,144,1152]{2,1,0:T(8,128)(2,1)} custom-call(bf16[512,2048]{1,0:T(8,128)(2,1)} %get-tuple-element.50.h_ref, bf16[512,640]{1,0:T(8,128)(2,1)} %get-tuple-element.51.right_ref, bf16[512,2048]{1,0:T(8,128)(2,1)} %copy.107.da_ref, bf16[4,512,128]{2,1,0:T(8,128)(2,1)} %get-tuple-element.45.o_ref, f32[16,2048]{1,0:T(8,128)} %select_maximum_fusion.gain_ref), custom_call_target="tpu_custom_call" | custom-call | tf_op jit(solution)/shard_map/attn_grads/pallas_call | solution.py:439
  409.8 4.6 all-to-all-start.2
  414.4 3.9 copy.109
  418.3 2.3 slice.139
  420.6 3.3 collective-permute-start.11
  423.8 3.9 copy.103
  427.7 1.4 slice.135
  429.7 1.7 add_convert_fusion.1
  431.4 1.3 collective-permute-start.12
  432.7 1.3 add_convert_fusion.4
  434.7 21.6 %collective-permute-done.12 = bf16[256,2048]{0,1:T(8,128)(2,1)S(1)} collective-permute-done((bf16[256,2048]{0,1:T(8,128)(2,1)S(1)}, bf16[256,2048]{0,1:T(8,128)(2,1)S(1)}, u32[]{:S(2)}, u32[]{:S(2)}) %collective-permute-start.12) | collective-permute-done | bytes 1048608 | tf_op jit(solution)/shard_map/ppermute | solution.py:533
  457.3 29.1 %all-to-all-done.2 = bf16[16,144,1152]{2,1,0:T(8,128)(2,1)} async-done(((bf16[16,144,1152]{2,1,0:T(8,128)(2,1)}), bf16[16,144,1152]{2,1,0:T(8,128)(2,1)}, u32[]{:S(2)}, u32[]{:S(2)}) %all-to-all-start.2) | async-done | bytes 5308448 | tf_op jit(solution)/shard_map/all_to_all | solution.py:638
  486.4 3.4 reduce_sum.72
  489.8 2.6 collective-permute-start.13
  492.4 5.0 fusion.5
  497.4 3.0 copy.123
  500.4 1.4 copy.122
  502.9 4.9 collective-permute-start.14
  507.8 1.2 collective-permute-done.14
  509.2 2.1 collective-permute-start.15
  511.7 24.0 %collective-permute-done.15 = bf16[128,4224]{1,0:T(8,128)(2,1)S(1)} collective-permute-done((bf16[128,4224]{1,0:T(8,128)(2,1)}, bf16[128,4224]{1,0:T(8,128)(2,1)S(1)}, u32[]{:S(2)}, u32[]{:S(2)}) %collective-permute-start.15) | collective-permute-done | bytes 1081376 | tf_op jit(solution)/shard_map/ppermute | solution.py:529
  536.0 1.6 collective-permute-start.16
  537.7 1.4 multiply_subtract_fusion
  539.1 1.4 multiply_subtract_fusion.1
  544.6 22.7 %mlp_adam.1 = (f32[128,2,2816]{2,1,0:T(2,128)}, f32[128,2,2816]{2,1,0:T(2,128)}, f32[128,2,2816]{2,1,0:T(2,128)}, f32[128,2816]{1,0:T(8,128)}, f32[128,2816]{1,0:T(8,128)}, /*index=5*/f32[128,2816]{1,0:T(8,128)}) custom-call(s32[1]{0:T(128)} %bitcast.9.core_ref, bf16[128,4224]{1,0:T(8,128)(2,1)} %copy-done.6, bf16[128,4224]{1,0:T(8,128)(2,1)} %copy-done.13, ...), custom_call_target="tpu_custom_call" | custom-call | tf_op jit(solution)/shard_map/mlp_adam/pallas_call | solution.py:513
  (120 shorter events, 20.6 us)
Async XLA Ops:
  7.2 64.0 %all-gather.6.cloned.1.call-start = ((), (), s32[]{:S(2)}) async-start(), calls=%async_computation.6 | async-start | bytes 5640192 | tf_op jit(solution)/shard_map/all_gather | solution.py:587
  11.1 201.4 %all-gather.4.cloned.1.call-start = ((), (), s32[]{:S(2)}) async-start(), calls=%async_computation.4 | async-start | bytes 18382848 | tf_op jit(solution)/shard_map/all_gather | solution.py:588
  11.1 7.5 %copy-start.8 = (bf16[2,128,2048]{2,1,0:T(8,128)(2,1)S(1)}, bf16[2,128,2048]{2,1,0:T(8,128)(2,1)}, u32[]{:S(2)}) copy-start(bf16[2,128,2048]{2,1,0:T(8,128)(2,1)} %param.21) | copy-start | bytes 3145732
  18.6 2.1 copy-start.23
  18.6 490.5 %reduce-scatter.2.cloned.1.call-start = ((), (), s32[]{:S(2)}) async-start(), calls=%async_computation.5 | async-start | bytes 18382848 | tf_op jit(solution)/shard_map/reduce_scatter | solution.py:623
  19.2 6.2 %collective-permute-start.1 = (bf16[256,2048]{0,1:T(8,128)(2,1)S(1)}, bf16[256,2048]{0,1:T(8,128)(2,1)}, u32[]{:S(2)}, u32[]{:S(2)}) collective-permute-start(bf16[256,2048]{0,1:T(8,128)(2,1)S(1)} %copy.120), channel_id=1, source_target_pairs={{0,32},{32,0},{64,96},{96,64},{1,33},{33,1},{65,97},{97,65},{2,34}... | collective-permute-start | bytes 3145736 | tf_op jit(solution)/shard_map/ppermute | solution.py:525
  20.7 2.1 collective-permute-start
  22.9 3.9 copy-start.22
  163.1 3.6 collective-permute-start.2
  167.9 24.7 %collective-permute-start.3 = (bf16[256,2048]{0,1:T(8,128)(2,1)}, bf16[256,2048]{0,1:T(8,128)(2,1)}, u32[]{:S(2)}, u32[]{:S(2)}) collective-permute-start(bf16[256,2048]{0,1:T(8,128)(2,1)} %add_convert_fusion.5), channel_id=1, source_target_pairs={{0,1},{1,0},{2,3},{3,2},{4,5},{5,4},{6,7},{7,6},{8,9},{9,8},{10,11... | collective-permute-start | bytes 3145736 | tf_op jit(solution)/shard_map/ppermute | solution.py:533
  171.4 25.8 %collective-permute-start.5 = (bf16[256,2048]{0,1:T(8,128)(2,1)}, bf16[256,2048]{0,1:T(8,128)(2,1)S(1)}, u32[]{:S(2)}, u32[]{:S(2)}) collective-permute-start(bf16[256,2048]{0,1:T(8,128)(2,1)} %copy.121), channel_id=1, source_target_pairs={{0,32},{32,0},{64,96},{96,64},{1,33},{33,1},{65,97},{97,65},{2,34}... | collective-permute-start | bytes 3145736 | tf_op jit(solution)/shard_map/ppermute | solution.py:525
  196.0 8.7 %collective-permute-start.4 = (bf16[256,2048]{0,1:T(8,128)(2,1)}, bf16[256,2048]{0,1:T(8,128)(2,1)}, u32[]{:S(2)}, u32[]{:S(2)}) collective-permute-start(bf16[256,2048]{0,1:T(8,128)(2,1)} %multiply_convert_fusion), channel_id=1, source_target_pairs={{0,32},{32,0},{64,96},{96,64},{1,33},{33,1},{65,97},{97,65},{2,34}... | collective-permute-start | bytes 3145736 | tf_op jit(solution)/shard_map/ppermute | solution.py:525
  266.2 4.2 copy-start.5
  267.6 2.7 collective-permute-start.8
  270.7 25.7 %copy-start = (bf16[256,2048]{0,1:T(8,128)(2,1)}, bf16[256,2048]{0,1:T(8,128)(2,1)S(1)}, u32[]{:S(2)}) copy-start(bf16[256,2048]{0,1:T(8,128)(2,1)S(1)} %add_convert_fusion.2) | copy-start | bytes 3145732
  270.7 24.8 %collective-permute-start.9 = (bf16[256,2048]{0,1:T(8,128)(2,1)S(1)}, bf16[256,2048]{0,1:T(8,128)(2,1)S(1)}, u32[]{:S(2)}, u32[]{:S(2)}) collective-permute-start(bf16[256,2048]{0,1:T(8,128)(2,1)S(1)} %add_convert_fusion.2), channel_id=1, source_target_pairs={{0,1},{1,0},{2,3},{3,2},{4,5},{5,4},{6,7},{7,6},{8,9},{9,8},{10,11... | collective-permute-start | bytes 3145736 | tf_op jit(solution)/shard_map/ppermute | solution.py:533
  295.5 1.0 copy-start.2
  298.5 3.2 collective-permute-start.10
  340.6 46.0 %all-to-all-start.1 = ((bf16[16,512,128]{2,1,0:T(8,128)(2,1)}), bf16[16,512,128]{2,1,0:T(8,128)(2,1)}, u32[]{:S(2)}, u32[]{:S(2)}) async-start(bf16[16,512,128]{2,1,0:T(8,128)(2,1)} %get-tuple-element.48), calls=%async_computation.1 | async-start | bytes 4194304 | tf_op jit(solution)/shard_map/all_to_all | solution.py:633
  409.8 76.6 %all-to-all-start.2 = ((bf16[16,144,1152]{2,1,0:T(8,128)(2,1)}), bf16[16,144,1152]{2,1,0:T(8,128)(2,1)}, u32[]{:S(2)}, u32[]{:S(2)}) async-start(bf16[16,144,1152]{2,1,0:T(8,128)(2,1)} %attn_grads.1), calls=%async_computation.2 | async-start | bytes 10616832 | tf_op jit(solution)/shard_map/all_to_all | solution.py:638
  420.6 8.7 %collective-permute-start.11 = (bf16[256,2048]{0,1:T(8,128)(2,1)}, bf16[256,2048]{0,1:T(8,128)(2,1)}, u32[]{:S(2)}, u32[]{:S(2)}) collective-permute-start(bf16[256,2048]{0,1:T(8,128)(2,1)} %slice.139), channel_id=1, source_target_pairs={{0,32},{32,0},{64,96},{96,64},{1,33},{33,1},{65,97},{97,65},{2,34}... | collective-permute-start | bytes 3145736 | tf_op jit(solution)/shard_map/ppermute | solution.py:525
  427.7 1.9 copy-start.4
  429.2 3.5 copy-start.3
  429.2 3.5 collective-permute-start.6
  431.4 25.0 %copy-start.1 = (bf16[256,2048]{0,1:T(8,128)(2,1)}, bf16[256,2048]{0,1:T(8,128)(2,1)S(1)}, u32[]{:S(2)}) copy-start(bf16[256,2048]{0,1:T(8,128)(2,1)S(1)} %add_convert_fusion.1) | copy-start | bytes 3145732
  431.4 3.1 copy-start.9
  431.4 25.0 %collective-permute-start.12 = (bf16[256,2048]{0,1:T(8,128)(2,1)S(1)}, bf16[256,2048]{0,1:T(8,128)(2,1)S(1)}, u32[]{:S(2)}, u32[]{:S(2)}) collective-permute-start(bf16[256,2048]{0,1:T(8,128)(2,1)S(1)} %add_convert_fusion.1), channel_id=1, source_target_pairs={{0,1},{1,0},{2,3},{3,2},{4,5},{5,4},{6,7},{7,6},{8,9},{9,8},{10,11... | collective-permute-start | bytes 3145736 | tf_op jit(solution)/shard_map/ppermute | solution.py:533
  434.0 58.4 %collective-permute-start.7 = (bf16[256,2048]{0,1:T(8,128)(2,1)}, bf16[256,2048]{0,1:T(8,128)(2,1)}, u32[]{:S(2)}, u32[]{:S(2)}) collective-permute-start(bf16[256,2048]{0,1:T(8,128)(2,1)} %add_convert_fusion.4), channel_id=1, source_target_pairs={{0,1},{1,0},{2,3},{3,2},{4,5},{5,4},{6,7},{7,6},{8,9},{9,8},{10,11... | collective-permute-start | bytes 3145736 | tf_op jit(solution)/shard_map/ppermute | solution.py:533
  456.4 1.0 copy-start.10
  489.8 12.0 %collective-permute-start.13 = (bf16[144,1152]{1,0:T(8,128)(2,1)S(1)}, bf16[144,1152]{1,0:T(8,128)(2,1)}, u32[]{:S(2)}, u32[]{:S(2)}) collective-permute-start(bf16[144,1152]{1,0:T(8,128)(2,1)S(1)} %reduce_sum.72), channel_id=1, source_target_pairs={{0,64},{32,96},{64,0},{96,32},{1,65},{33,97},{65,1},{97,33},{2,66}... | collective-permute-start | bytes 995336 | tf_op jit(solution)/shard_map/ppermute | solution.py:529
  497.4 3.0 copy-start.7
  502.9 6.1 %collective-permute-start.14 = (bf16[144,1152]{1,0:T(8,128)(2,1)S(1)}, bf16[144,1152]{1,0:T(8,128)(2,1)S(1)}, u32[]{:S(2)}, u32[]{:S(2)}) collective-permute-start(bf16[144,1152]{1,0:T(8,128)(2,1)S(1)} %add_convert_fusion.6), channel_id=1, source_target_pairs={{0,32},{32,0},{64,96},{96,64},{1,33},{33,1},{65,97},{97,65},{2,34}... | collective-permute-start | bytes 995336 | tf_op jit(solution)/shard_map/ppermute | solution.py:525
  509.0 34.0 %collective-permute-start.17 = (f32[2,128]{1,0:T(2,128)S(1)}, f32[2,128]{1,0:T(2,128)S(1)}, u32[]{:S(2)}, u32[]{:S(2)}) collective-permute-start(f32[2,128]{1,0:T(2,128)S(1)} %convert_add_fusion.2), channel_id=1, source_target_pairs={{0,1},{1,0},{2,3},{3,2},{4,5},{5,4},{6,7},{7,6},{8,9},{9,8},{10,11... | collective-permute-start | bytes 3080 | tf_op jit(solution)/shard_map/ppermute | solution.py:533
  509.2 26.5 %copy-start.14 = (bf16[128,4224]{1,0:T(8,128)(2,1)S(1)}, bf16[128,4224]{1,0:T(8,128)(2,1)}, u32[]{:S(2)}) copy-start(bf16[128,4224]{1,0:T(8,128)(2,1)} %reduce-scatter.2.cloned.1.call-done) | copy-start | bytes 3244036
  509.2 26.5 %collective-permute-start.15 = (bf16[128,4224]{1,0:T(8,128)(2,1)}, bf16[128,4224]{1,0:T(8,128)(2,1)S(1)}, u32[]{:S(2)}, u32[]{:S(2)}) collective-permute-start(bf16[128,4224]{1,0:T(8,128)(2,1)} %reduce-scatter.2.cloned.1.call-done), channel_id=1, source_target_pairs={{0,64},{32,96},{64,0},{96,32},{1,65},{33,97},{65,1},{97,33},{2,66}... | collective-permute-start | bytes 3244040 | tf_op jit(solution)/shard_map/ppermute | solution.py:529
  511.7 26.0 %copy-start.11 = (f32[128,1024]{1,0:T(8,128)S(1)}, f32[128,1024]{1,0:T(8,128)}, u32[]{:S(2)}) copy-start(f32[128,1024]{1,0:T(8,128)} %param.30) | copy-start | bytes 1572868
  511.7 26.0 %copy-start.15 = (f32[128,1024]{1,0:T(8,128)S(1)}, f32[128,1024]{1,0:T(8,128)}, u32[]{:S(2)}) copy-start(f32[128,1024]{1,0:T(8,128)} %param.31) | copy-start | bytes 1572868
  511.7 26.0 %copy-start.16 = (f32[128,1024]{1,0:T(8,128)S(1)}, f32[128,1024]{1,0:T(8,128)}, u32[]{:S(2)}) copy-start(f32[128,1024]{1,0:T(8,128)} %param.32) | copy-start | bytes 1572868
  535.9 4.6 copy-start.6
  535.9 3.2 copy-start.12
  535.9 3.2 copy-start.17
  535.9 3.2 copy-start.18
  536.0 7.6 %collective-permute-start.16 = (bf16[128,4224]{1,0:T(8,128)(2,1)S(1)}, bf16[128,4224]{1,0:T(8,128)(2,1)S(1)}, u32[]{:S(2)}, u32[]{:S(2)}) collective-permute-start(bf16[128,4224]{1,0:T(8,128)(2,1)S(1)} %add_convert_fusion.own_ref), channel_id=1, source_target_pairs={{0,32},{32,0},{64,96},{96,64},{1,33},{33,1},{65,97},{97,65},{2,34}... | collective-permute-start | bytes 3244040 | tf_op jit(solution)/shard_map/ppermute | solution.py:525
  539.1 1.5 copy-start.19
  539.1 1.5 copy-start.20
  539.1 1.5 copy-start.21
  539.1 3.9 copy-start.24
  539.1 3.8 copy-start.25
  539.1 3.8 copy-start.26
  543.6 1.0 copy-start.13
Sparse Core Ops, SparseCore 0:
  11.2 59.9 all-gather.5
  73.9 134.8 all-gather.3
  262.4 129.4 reduce-scatter.1
